TPU v7x, 128 devices: a whole 4x4x4 slice. The times are simulated.
128 devices in a mesh: freq: 8 (over x, core), tile: 16 (over y, z).
Axes of the slice: x: 4, y: 4, z: 4, core: 2. Of those that a mesh axis runs over, the one named last changes fastest.
Arguments:
- plus_time: bfloat16 [128, 128, 12288], P('freq', None, 'tile'), may hold values from -6 to 6
- minus_time: bfloat16 [128, 128, 12288], P('freq', None, 'tile'), may hold values from -6 to 6
- gate_starts: int32 [128, 48], P('freq', 'tile'), may hold values from 0 to 64
- tile_ranks: int32 [8, 48, 48], P('freq', None, 'tile'), may hold values from 1 to 64, as said below
- u_factors: bfloat16 [8, 48, 48, 2, 64, 256], P('freq', 'tile'), may hold values from -0.109375 to 0.109375
- v_factors: bfloat16 [8, 48, 48, 2, 64, 256], P('freq', None, 'tile'), may hold values from -0.375 to 0.375
Outputs:
- minus_new: bfloat16 [8, 2, 128, 12288], P('freq', None, None, 'tile')
- plus_new: bfloat16 [8, 2, 128, 12288], P('freq', None, None, 'tile')
- cross_gram: float32 [8, 2, 128, 128], P('freq', None, 'tile')
- normal_gram: float32 [8, 2, 128, 128], P('freq', None, 'tile')
Inputs may be any that keep to these rules, and one draw needn't show every extreme that they name: `tile_ranks`: tiles with |i - j| <= 1 have rank 64; every other tile has rank at most 32, and some tile of every draw has exactly 32.
All inputs are finite; a program needn't handle non-finite values.
Results may differ from a plain program's by a relative error of at most 0.014.
Values may be sent and summed in bfloat16 or wider, within the bound.
No kernel may reach another device: no remote copies, remote signals or barrier semaphores. Data moves between devices by JAX's collectives and lax.ppermute only.
A program may use at most 192 MiB of HBM per device.

v0:
```python
import math

import jax
import jax.numpy as jnp
from jax import lax
from jax.sharding import Mesh
from jax.sharding import PartitionSpec as P

R = 12288
GATE = 64
FREQ = ("freq_0", "freq_1")


def cut_along(x, dim, size):
    dims = x.shape
    parts = x.reshape(*dims[:dim], size, dims[dim] // size, *dims[dim + 1 :])
    return jnp.moveaxis(parts, dim, 0)


def laid_out(parts, dim):
    dims = list(parts.shape[1:])
    dims[dim] *= parts.shape[0]
    return jnp.moveaxis(parts, 0, dim).reshape(dims)


def turned_blocks(parts, axes, turns):
    dims = [lax.axis_size(a) for a in axes]
    parts = parts.reshape(*dims, *parts.shape[1:])
    for k in turns:
        parts = lax.all_to_all(parts, axes[k], split_axis=k, concat_axis=k, tiled=True)
    return parts.reshape(-1, *parts.shape[len(axes) :])


def stepwise_exchange(x, axes, turns, split_dim, concat_dim):
    parts = cut_along(x, split_dim, lax.axis_size(axes))
    return laid_out(turned_blocks(parts, axes, turns), concat_dim)


def extended(x, sides, width):
    for axis, dim in sides:
        size, length = (lax.axis_size(axis), x.shape[dim])
        up = [(i, (i + 1) % size) for i in range(size - 1)]
        down = [(j, i) for i, j in up]
        last = lax.slice_in_dim(x, length - width, length, axis=dim)
        leading = lax.slice_in_dim(x, 0, width, axis=dim)
        before = lax.ppermute(last, axis, up)
        after = lax.ppermute(leading, axis, down)
        x = jnp.concatenate([before, x, after], axis=dim)
    return x


def summed_on_arrival(x, axis, dim):
    parts = cut_along(x, dim, lax.axis_size(axis))
    arrived = lax.all_to_all(parts, axis, split_axis=0, concat_axis=0, tiled=True)
    return arrived.astype(jnp.float32).sum(axis=0)


def make_table(freq_count, sample_count):
    freq_ids = lax.broadcasted_iota(jnp.int32, (freq_count, sample_count), 0)
    sample_ids = lax.broadcasted_iota(jnp.int32, (freq_count, sample_count), 1)
    phase_ids = freq_ids * sample_ids % sample_count
    angles = phase_ids.astype(jnp.float32) * (2.0 * math.pi / sample_count)
    amplitude = 1.0 / math.sqrt(GATE)
    return jnp.stack([jnp.cos(angles) * amplitude, -jnp.sin(angles) * amplitude]).astype(
        jnp.bfloat16
    )


def half_signs(entry_count):
    entry_ids = lax.broadcasted_iota(jnp.int32, (entry_count,), 0)
    return jnp.where(entry_ids < entry_count // 2, 1.0, -1.0).astype(jnp.float32)


def gate_field(traces, gate_starts):
    sources, samples, receivers = traces.shape
    blocks = gate_starts.shape[1]
    shaped = traces.reshape(sources, samples, blocks, receivers // blocks)
    sample_ids = lax.broadcasted_iota(jnp.int32, (1, samples, 1, 1), 1)
    starts = gate_starts[:, None, :, None]
    inside = (sample_ids >= starts) & (sample_ids < starts + GATE)
    kept = jnp.where(inside, shaped, jnp.zeros((), traces.dtype))
    return kept.reshape(sources, samples, receivers)


def on_device(plus_time, minus_time, gate_starts, tile_ranks, u_factors, v_factors):
    f_local = u_factors.shape[0]
    row_tiles = u_factors.shape[1]
    all_tiles = u_factors.shape[2]
    col_tiles = v_factors.shape[2]
    rank_depth = v_factors.shape[4]
    half_depth = rank_depth // 2
    freq_total = f_local * lax.axis_size(FREQ)
    sample_count = plus_time.shape[1]
    stacked = jnp.stack([gate_field(plus_time, gate_starts), gate_field(minus_time, gate_starts)])
    dft_table = make_table(freq_total, sample_count)
    local_spec = jnp.einsum(
        "cft,qstr->fcqsr", dft_table, stacked, preferred_element_type=jnp.float32
    ).astype(jnp.bfloat16)
    spectra = stepwise_exchange(local_spec, FREQ, (1, 0), 0, 3)
    both_sources = 2 * spectra.shape[3]
    columns = spectra.reshape(f_local, 2, both_sources, col_tiles, spectra.shape[4] // col_tiles)
    sign_vec = half_signs(both_sources)
    partial_c = jnp.einsum(
        "fijckr,fdsjr->fijcdks", v_factors, columns, preferred_element_type=jnp.float32
    )
    coeff_real = partial_c[:, :, :, 0, 0] - sign_vec * partial_c[:, :, :, 1, 1]
    coeff_imag = partial_c[:, :, :, 0, 1] + sign_vec * partial_c[:, :, :, 1, 0]
    rank_ids = lax.broadcasted_iota(jnp.int32, (1, 1, 1, rank_depth), 3)
    rank_mask = (rank_ids < tile_ranks[:, :, :, None]).astype(jnp.float32)[..., None]
    coeff_all = jnp.stack([coeff_real * rank_mask, coeff_imag * rank_mask], 3).astype(jnp.bfloat16)
    lower_part = coeff_all[:, :, :, :, :half_depth]
    lower_rows = lax.all_to_all(lower_part, "tile", split_axis=1, concat_axis=2, tiled=True)
    products = jnp.einsum(
        "fijckr,fijeks->fcesir",
        u_factors[:, :, :, :, :half_depth],
        lower_rows,
        preferred_element_type=jnp.float32,
    )
    block_start = lax.axis_index("tile") * col_tiles
    local_ids = lax.broadcasted_iota(jnp.int32, (col_tiles,), 0)
    global_cols = block_start + local_ids
    band_list = []
    for offset in (-1, 0, 1):
        band_rows = global_cols + offset
        valid = (band_rows >= 0) & (band_rows < all_tiles)
        clipped = jnp.clip(band_rows, 0, all_tiles - 1)
        picked = coeff_all[:, clipped, local_ids][:, :, :, half_depth:]
        band_list.append(
            jnp.where(valid[None, :, None, None, None], picked, jnp.zeros((), picked.dtype))
        )
    band_upper = jnp.stack(band_list, 1)
    padded_band = extended(band_upper, (("tile", 2),), 1)
    row_global = lax.axis_index("tile") * row_tiles + lax.broadcasted_iota(
        jnp.int32, (row_tiles,), 0
    )
    row_local = lax.broadcasted_iota(jnp.int32, (row_tiles,), 0)
    coeff_band = []
    u_band = []
    for position, offset in enumerate((-1, 0, 1)):
        coeff_band.append(padded_band[:, position, 1 - offset : 1 - offset + row_tiles])
        partner = jnp.clip(row_global - offset, 0, all_tiles - 1)
        u_band.append(u_factors[:, row_local, partner][:, :, :, half_depth:])
    band_products = jnp.einsum(
        "fdickr,fdieks->fcesir",
        jnp.stack(u_band, 1),
        jnp.stack(coeff_band, 1),
        preferred_element_type=jnp.float32,
    )
    products = products + band_products
    resp_real = products[:, 0, 0] - sign_vec[:, None, None] * products[:, 1, 1]
    resp_imag = products[:, 0, 1] + sign_vec[:, None, None] * products[:, 1, 0]
    response = jnp.stack([resp_real, resp_imag], 1).reshape(f_local, 2, both_sources, -1)
    rounded = response.astype(jnp.bfloat16)
    half_count = both_sources // 2
    minus_new = rounded[:, :, :half_count]
    plus_new = rounded[:, :, half_count:]
    gram_parts = jnp.einsum(
        "fczr,fesr->fczes", rounded, plus_new, preferred_element_type=jnp.float32
    )
    gram_real = gram_parts[:, 0, :, 0] + gram_parts[:, 1, :, 1]
    gram_imag = gram_parts[:, 1, :, 0] - gram_parts[:, 0, :, 1]
    row_ids = lax.broadcasted_iota(jnp.int32, (both_sources, 1), 0)
    row_scale = jnp.where(row_ids < half_count, 1.0 / math.sqrt(R), 1.0 / R).astype(jnp.float32)
    gram_all = jnp.stack([gram_real * row_scale, gram_imag * row_scale], 1)
    gram_all = gram_all.reshape(f_local, 2, 2, half_count, half_count).transpose(0, 2, 1, 3, 4)
    own_rows = summed_on_arrival(gram_all.astype(jnp.bfloat16), "tile", 3)
    return (minus_new, plus_new, own_rows[:, 0], own_rows[:, 1])


def solution(mesh):
    torus = Mesh(mesh.devices.reshape(4, 2, mesh.shape["tile"]), ("freq_0", "freq_1", "tile"))
    in_specs = (
        P(FREQ, None, "tile"),
        P(FREQ, None, "tile"),
        P(FREQ, "tile"),
        P(FREQ, None, "tile"),
        P(FREQ, "tile", None, None, None, None),
        P(FREQ, None, "tile", None, None, None),
    )
    out_specs = (
        P(FREQ, None, None, "tile"),
        P(FREQ, None, None, "tile"),
        P(FREQ, None, "tile", None),
        P(FREQ, None, "tile", None),
    )
    return jax.shard_map(
        on_device, mesh=torus, in_specs=in_specs, out_specs=out_specs, check_vma=False
    )
```

profile of v0, /device:TPU:0, one launch (start us, length us, event | category | flops | bytes accessed | tf_op | source)
XLA Modules:
  0.0 175.1 jit_solution(7365686734960798835)
XLA Ops:
  0.6 0.7 broadcast_add_fusion
  1.3 0.8 copy.61
  2.1 0.1 multiply_convert_fusion.2
  2.1 0.1 copy.62
  2.2 0.1 fusion.50
  2.3 0.4 broadcast_in_dim.81
  2.7 2.5 %copy.63 = pred[16,128,768]{2,1,0:T(8,128)(4,1)S(1)} copy(pred[16,128,768]{1,2,0:T(8,128)(4,1)S(1)} %bitcast.194) | data formatting | bytes 3145728 | tf_op jit(solution)/shard_map/jit(_where)/broadcast_in_dim | solution.py:81
  5.2 3.4 %select_bitcast_fusion.1 = (bf16[1,16,128,768]{3,2,1,0:T(8,128)(2,1)S(1)}, bf16[1,16,128,768]{3,2,1,0:T(8,128)(2,1)S(1)}) fusion(pred[16,128,768]{2,1,0:T(8,128)(4,1)S(1)} %copy.63, bf16[16,128,768]{2,1,0:T(8,128)(2,1)} %param.6, bf16[16,128,768]{2,1,0:T(8,128)(2,1)} %param.7), kind=kLoop, calls=%fused_computation.37 | loop fusion | flops 3145728 | bytes 14155776 | tf_op jit(solution)/shard_map/jit(_where)/select_n | solution.py:81
  8.6 1.1 fusion.20
  9.7 0.0 copy-start.4
  9.7 0.3 reshape_reshape.4
  10.0 0.3 copy.65
  10.3 4.4 %all_to_all.30 = bf16[4,2,1,2,2,16,768]{6,0,3,5,4,2,1:T(4,128)(2,1)S(1)} all-to-all(bf16[4,2,1,2,2,16,768]{6,0,3,5,4,2,1:T(4,128)(2,1)S(1)} %copy.65), channel_id=1, replica_groups=mesh['freq_0'=4,'freq_1'=2,'tile'=16] {'freq_1'}, dimensions={1} | all-to-all | bytes 1572864 | tf_op jit(solution)/shard_map/all_to_all | solution.py:30
  14.7 1.7 copy.66
  16.4 4.4 %all-to-all-start.1 = ((bf16[4,2,1,2,2,16,768]{6,1,3,5,4,2,0:T(2,128)(2,1)}), bf16[4,2,1,2,2,16,768]{6,1,3,5,4,2,0:T(2,128)(2,1)S(1)}, u32[]{:S(2)}, u32[]{:S(2)}) async-start(bf16[4,2,1,2,2,16,768]{6,1,3,5,4,2,0:T(2,128)(2,1)} %copy.66), calls=%async_computation.1 | async-start | bytes 1572864 | tf_op jit(solution)/shard_map/all_to_all | solution.py:30
  20.8 0.0 copy-done.4
  20.8 0.1 fusion.49
  20.9 12.5 %all-to-all-done.1 = bf16[4,2,1,2,2,16,768]{6,1,3,5,4,2,0:T(2,128)(2,1)S(1)} async-done(((bf16[4,2,1,2,2,16,768]{6,1,3,5,4,2,0:T(2,128)(2,1)}), bf16[4,2,1,2,2,16,768]{6,1,3,5,4,2,0:T(2,128)(2,1)S(1)}, u32[]{:S(2)}, u32[]{:S(2)}) %all-to-all-start.1) | async-done | bytes 786464 | tf_op jit(solution)/shard_map/all_to_all | solution.py:30
  33.4 0.1 copy.67
  33.5 0.1 copy.68
  33.6 0.4 reshape.604
  33.9 17.3 %convolution_bitcast_fusion = f32[1,48,3,2,2,64,256]{6,5,3,1,4,2,0:T(8,128)} fusion(bf16[2,256,3,256,1,1]{3,2,1,0,5,4:T(4,128)(2,1)S(1)} %bitcast.196, bf16[1,48,3,2,64,256]{5,4,3,2,1,0:T(8,128)(2,1)} %param.11), kind=kOutput, calls=%fused_computation.6 | convolution fusion | flops 4831838208 | bytes 47972352 | tf_op jit(solution)/shard_map/fijckr,fdsjr->fijcdks/dot_general | solution.py:103
  51.2 13.1 %fusion.14 = (bf16[1,48,3,1,64,256]{5,4,1,2,3,0:T(8,128)(2,1)S(1)}, bf16[1,48,3,1,64,256]{5,4,1,2,3,0:T(8,128)(2,1)S(1)}) fusion(f32[1,48,3,2,2,64,256]{6,5,3,1,4,2,0:T(8,128)} %convolution_bitcast_fusion, f32[48,3,64]{2,0,1:T(8,128)S(1)} %fusion.49, f32[256]{0:T(256)S(1)} %compare_select_fusion.4), kind=kLoop, calls=%fused_computation.29 | loop fusion | flops 18874368 | bytes 47223808 | tf_op jit(solution)/shard_map/stack | solution.py:110
  64.3 0.0 copy-start
  64.4 0.5 fusion.15
  64.8 1.7 copy-done
  66.5 1.5 copy-done.1
  68.0 2.7 %copy.74 = bf16[1,48,3,2,32,256]{5,4,2,3,0,1:T(8,128)(2,1)} copy(bf16[1,48,3,2,32,256]{5,4,1,2,3,0:T(8,128)(2,1)S(1)} %fusion.15) | data formatting | bytes 9437184 | tf_op jit(solution)/shard_map/slice | solution.py:111
  70.7 8.1 %all-to-all-start.2 = ((bf16[1,48,3,2,32,256]{5,4,2,3,0,1:T(8,128)(2,1)}), bf16[1,48,3,2,32,256]{5,4,2,3,0,1:T(8,128)(2,1)}, u32[]{:S(2)}, u32[]{:S(2)}) async-start(bf16[1,48,3,2,32,256]{5,4,2,3,0,1:T(8,128)(2,1)} %copy.74), calls=%async_computation.2 | async-start | bytes 9437184 | tf_op jit(solution)/shard_map/all_to_all | solution.py:112
  78.8 4.2 %gather_fusion.5 = bf16[3,2,64,256]{3,2,1,0:T(8,128)(2,1)S(1)} fusion(bf16[3,48,2,64,256]{4,3,2,1,0:T(8,128)(2,1)} %bitcast.213, s32[3]{0:T(128)S(1)} %get-tuple-element.28), kind=kCustom, calls=%fused_computation.5 | custom fusion | bytes 393240 | tf_op jit(solution)/shard_map/gather | solution.py:142
  83.1 4.2 %gather_fusion.4 = bf16[3,2,64,256]{3,2,1,0:T(8,128)(2,1)S(1)} fusion(bf16[3,48,2,64,256]{4,3,2,1,0:T(8,128)(2,1)} %bitcast.214, s32[3]{0:T(128)S(1)} %get-tuple-element.29), kind=kCustom, calls=%fused_computation.4 | custom fusion | bytes 393240 | tf_op jit(solution)/shard_map/gather | solution.py:142
  87.3 4.2 %gather_fusion.3 = bf16[3,2,64,256]{3,2,1,0:T(8,128)(2,1)S(1)} fusion(bf16[3,48,2,64,256]{4,3,2,1,0:T(8,128)(2,1)} %bitcast.215, s32[3]{0:T(128)S(1)} %get-tuple-element.30), kind=kCustom, calls=%fused_computation.3 | custom fusion | bytes 393240 | tf_op jit(solution)/shard_map/gather | solution.py:142
  91.7 8.3 %fusion = bf16[48,3,2,64,256]{4,3,0,1,2:T(8,128)(2,1)} fusion(bf16[1,48,3,1,64,256]{5,4,1,2,3,0:T(8,128)(2,1)} %copy-done, bf16[1,48,3,1,64,256]{5,4,1,2,3,0:T(8,128)(2,1)} %copy-done.1), kind=kLoop, calls=%fused_computation.10 | loop fusion | flops 4718592 | bytes 18874368 | tf_op jit(solution)/shard_map/stack | solution.py:110
  100.0 4.2 %gather_fusion.2 = bf16[3,2,64,256]{3,2,1,0:T(8,128)(2,1)S(1)} fusion(bf16[48,3,2,64,256]{4,3,0,1,2:T(8,128)(2,1)} %fusion, s32[3]{0:T(128)S(1)} %get-tuple-element.31), kind=kCustom, calls=%fused_computation.2 | custom fusion | bytes 393240 | tf_op jit(solution)/shard_map/gather | solution.py:127
  104.3 4.2 %gather_fusion.1 = bf16[3,2,64,256]{3,2,1,0:T(8,128)(2,1)S(1)} fusion(bf16[48,3,2,64,256]{4,3,0,1,2:T(8,128)(2,1)} %fusion, s32[3]{0:T(128)S(1)} %get-tuple-element.32), kind=kCustom, calls=%fused_computation.1 | custom fusion | bytes 393240 | tf_op jit(solution)/shard_map/gather | solution.py:127
  108.5 4.2 %gather_fusion = bf16[3,2,64,256]{3,2,1,0:T(8,128)(2,1)S(1)} fusion(bf16[48,3,2,64,256]{4,3,0,1,2:T(8,128)(2,1)} %fusion, s32[3]{0:T(128)S(1)} %get-tuple-element.33), kind=kCustom, calls=%fused_computation | custom fusion | bytes 393240 | tf_op jit(solution)/shard_map/gather | solution.py:127
  112.8 0.1 fusion.46
  112.8 0.1 fusion.47
  112.9 0.1 fusion.48
  113.1 1.3 collective-permute-start
  114.4 4.7 %collective-permute-start.1 = (bf16[1,3,1,2,32,256]{5,4,3,2,1,0:T(8,128)(2,1)S(1)}, bf16[1,3,1,2,32,256]{5,4,3,2,1,0:T(8,128)(2,1)S(1)}, u32[]{:S(2)}, u32[]{:S(2)}) collective-permute-start(bf16[1,3,1,2,32,256]{5,4,3,2,1,0:T(8,128)(2,1)S(1)} %get-tuple-element.17), channel_id=1, source_target_pairs={{0,1},{1,2},{2,3},{3,4},{4,5},{5,6},{6,7},{7,8},{8,9},{9,10},{10,1... | collective-permute-start | bytes 294920 | tf_op jit(solution)/shard_map/ppermute | solution.py:46
  119.1 20.2 %all-to-all-done.2 = bf16[1,48,3,2,32,256]{5,4,2,3,0,1:T(8,128)(2,1)} async-done(((bf16[1,48,3,2,32,256]{5,4,2,3,0,1:T(8,128)(2,1)}), bf16[1,48,3,2,32,256]{5,4,2,3,0,1:T(8,128)(2,1)}, u32[]{:S(2)}, u32[]{:S(2)}) %all-to-all-start.2) | async-done | bytes 4718624 | tf_op jit(solution)/shard_map/all_to_all | solution.py:112
  139.3 3.1 %copy.75 = bf16[1,48,3,2,32,256]{5,4,3,2,1,0:T(8,128)(2,1)S(1)} copy(bf16[1,48,3,2,32,256]{5,4,2,3,0,1:T(8,128)(2,1)} %all-to-all-done.2) | data formatting | bytes 9437184 | tf_op jit(solution)/shard_map/all_to_all | solution.py:112
  142.4 0.0 slice-start.2
  142.4 0.5 copy.76
  143.0 1.2 slice-done.1
  144.2 0.4 slice-done.2
  144.6 2.6 %fusion.16 = f32[3,2,256,2,256,1]{2,4,5,3,1,0:T(8,128)S(1)} fusion(bf16[3,48,2,32,256,1]{4,3,2,1,0,5:T(8,128)(2,1)S(1)} %bitcast.195, bf16[1,3,48,2,64,256]{5,4,3,2,1,0:T(8,128)(2,1)S(1)} %bitcast.217), kind=kOutput, calls=%fused_computation.32 | convolution fusion | flops 2415919104 | bytes 12582912 | tf_op jit(solution)/shard_map/fijckr,fijeks->fcesir/dot_general | solution.py:113
  147.3 0.0 collective-permute-done
  147.3 0.0 collective-permute-done.1
  147.3 0.6 fusion.18
  147.9 0.4 fusion.67
  148.3 1.2 copy.80
  149.5 1.2 copy.81
  150.7 0.3 copy.82
  151.0 0.3 copy.83
  151.2 0.0 copy-done.2
  151.3 1.3 add_convert_fusion
  152.6 0.8 pad_maximum_fusion.1
  153.4 0.4 convolution_bitcast_fusion.1
  153.8 0.1 multiply_convert_fusion.1
  154.0 20.5 %all_to_all.31 = bf16[16,1,2,2,8,128]{5,4,2,3,1,0:T(8,128)(2,1)S(1)} all-to-all(bf16[16,1,2,2,8,128]{5,4,2,3,1,0:T(8,128)(2,1)S(1)} %copy.86), channel_id=1, replica_groups=mesh['freq_0'=4,'freq_1'=2,'tile'=16] {'tile'}, dimensions={0} | all-to-all | bytes 262144 | tf_op jit(solution)/shard_map/all_to_all | solution.py:54
  174.5 0.6 slice_bitcast_fusion.7
  175.1 0.0 copy-done.3
  (24 shorter events, 0.2 us)
Async XLA Ops:
  9.7 11.1 %copy-start.4 = (s32[1,48,3]{1,0,2:T(1,128)S(1)}, s32[1,48,3]{1,0,2:T(1,128)}, u32[]{:S(2)}) copy-start(s32[1,48,3]{1,0,2:T(1,128)} %param.9) | copy-start | bytes 1732
  16.4 17.0 %all-to-all-start.1 = ((bf16[4,2,1,2,2,16,768]{6,1,3,5,4,2,0:T(2,128)(2,1)}), bf16[4,2,1,2,2,16,768]{6,1,3,5,4,2,0:T(2,128)(2,1)S(1)}, u32[]{:S(2)}, u32[]{:S(2)}) async-start(bf16[4,2,1,2,2,16,768]{6,1,3,5,4,2,0:T(2,128)(2,1)} %copy.66), calls=%async_computation.1 | async-start | bytes 1572864 | tf_op jit(solution)/shard_map/all_to_all | solution.py:30
  64.3 2.2 %copy-start = (bf16[1,48,3,1,64,256]{5,4,1,2,3,0:T(8,128)(2,1)}, bf16[1,48,3,1,64,256]{5,4,1,2,3,0:T(8,128)(2,1)S(1)}, u32[]{:S(2)}) copy-start(bf16[1,48,3,1,64,256]{5,4,1,2,3,0:T(8,128)(2,1)S(1)} %get-tuple-element.4) | copy-start | bytes 14155780
  64.3 3.7 %copy-start.1 = (bf16[1,48,3,1,64,256]{5,4,1,2,3,0:T(8,128)(2,1)}, bf16[1,48,3,1,64,256]{5,4,1,2,3,0:T(8,128)(2,1)S(1)}, u32[]{:S(2)}) copy-start(bf16[1,48,3,1,64,256]{5,4,1,2,3,0:T(8,128)(2,1)S(1)} %get-tuple-element.5) | copy-start | bytes 14155780
  70.7 68.7 %all-to-all-start.2 = ((bf16[1,48,3,2,32,256]{5,4,2,3,0,1:T(8,128)(2,1)}), bf16[1,48,3,2,32,256]{5,4,2,3,0,1:T(8,128)(2,1)}, u32[]{:S(2)}, u32[]{:S(2)}) async-start(bf16[1,48,3,2,32,256]{5,4,2,3,0,1:T(8,128)(2,1)} %copy.74), calls=%async_computation.2 | async-start | bytes 9437184 | tf_op jit(solution)/shard_map/all_to_all | solution.py:112
  113.1 34.2 %collective-permute-start = (bf16[1,3,1,2,32,256]{5,4,3,2,1,0:T(8,128)(2,1)S(1)}, bf16[1,3,1,2,32,256]{5,4,3,2,1,0:T(8,128)(2,1)S(1)}, u32[]{:S(2)}, u32[]{:S(2)}) collective-permute-start(bf16[1,3,1,2,32,256]{5,4,3,2,1,0:T(8,128)(2,1)S(1)} %get-tuple-element.16), channel_id=1, source_target_pairs={{1,0},{2,1},{3,2},{4,3},{5,4},{6,5},{7,6},{8,7},{9,8},{10,9},{11,1... | collective-permute-start | bytes 294920 | tf_op jit(solution)/shard_map/ppermute | solution.py:47
  114.4 32.9 %collective-permute-start.1 = (bf16[1,3,1,2,32,256]{5,4,3,2,1,0:T(8,128)(2,1)S(1)}, bf16[1,3,1,2,32,256]{5,4,3,2,1,0:T(8,128)(2,1)S(1)}, u32[]{:S(2)}, u32[]{:S(2)}) collective-permute-start(bf16[1,3,1,2,32,256]{5,4,3,2,1,0:T(8,128)(2,1)S(1)} %get-tuple-element.17), channel_id=1, source_target_pairs={{0,1},{1,2},{2,3},{3,4},{4,5},{5,6},{6,7},{7,8},{8,9},{9,10},{10,1... | collective-permute-start | bytes 294920 | tf_op jit(solution)/shard_map/ppermute | solution.py:46
  139.3 3.7 %slice-start = ((s8[9437184]{0:T(1024)(128)(4,1)}), s8[4194304]{0:T(1024)(128)(4,1)S(1)}, s32[]{:S(2)}) async-start(s8[9437184]{0:T(1024)(128)(4,1)} %bitcast.216), calls=%async_computation.4 | async-start | bytes 8388608
  139.3 4.9 %slice-start.1 = ((s8[9437184]{0:T(1024)(128)(4,1)}), s8[4194304]{0:T(1024)(128)(4,1)S(1)}, s32[]{:S(2)}) async-start(s8[9437184]{0:T(1024)(128)(4,1)} %bitcast.216), calls=%async_computation.5 | async-start | bytes 8388608
  142.4 2.2 %slice-start.2 = ((s8[9437184]{0:T(1024)(128)(4,1)}), s8[1048576]{0:T(1024)(128)(4,1)S(1)}, s32[]{:S(2)}) async-start(s8[9437184]{0:T(1024)(128)(4,1)} %bitcast.216), calls=%async_computation.6 | async-start | bytes 2097152
  149.5 1.7 copy-start.2
  153.4 21.7 %copy-start.3 = (bf16[1,2,128,768]{3,2,1,0:T(8,128)(2,1)}, bf16[1,2,128,768]{3,2,1,0:T(8,128)(2,1)S(1)}, u32[]{:S(2)}) copy-start(bf16[1,2,128,768]{3,2,1,0:T(8,128)(2,1)S(1)} %get-tuple-element.12) | copy-start | bytes 1179652
where the time goes:
time: 176 us; the launch traced here: 175 us
  local copies, waits for them, and re-layouts  47.1 us (27%)
  waiting for transfers between devices  32.7 us (19%)
  other arithmetic  28.9 us (16%)
  blocking collectives  24.8 us (14%)
  matrix products  22 us (12%)
  starting transfers between devices  18.5 us (11%)
    another operation x3, other arithmetic, on_device(): jnp.stack([coeff_real * rank_mask, coeff_imag * rank_mask], 3)  21.9 us
    all_to_all x1, blocking collectives, summed_on_arrival(): lax.all_to_all(parts, axis, split_axis=0, concat_axis=0, tiled=True)  20.5 us
    all_to_all x1, waiting for transfers between devices, on_device(): lax.all_to_all(lower_part, 'tile', split_axis=1, concat_axis=2, tiled=True)  20.2 us
    dot_general x1, matrix products, on_device(): jnp.einsum('fijckr,fdsjr->fijcdks', v_factors, columns, preferred_element...  17.3 us
    gather x3, local copies, waits for them, and re-layouts, on_device(): u_band.append(u_factors[:, row_local, partner][:, :, :, half_depth:])  12.7 us
    gather x3, local copies, waits for them, and re-layouts, on_device(): picked = coeff_all[:, clipped, local_ids][:, :, :, half_depth:]  12.7 us
    all_to_all x1, waiting for transfers between devices, turned_blocks(): lax.all_to_all(parts, axes[k], split_axis=k, concat_axis=k, tiled=True)  12.5 us
    all_to_all x1, starting transfers between devices, on_device(): lax.all_to_all(lower_part, 'tile', split_axis=1, concat_axis=2, tiled=True)  8.09 us
  transfers between devices with their start and end apart: 4, of which 2 were waited for; matrix products, arithmetic and copies ran while one was open for 23% of the time, Pallas kernels for 0%

commit v1 on v0

v1 whole, which is shorter than its diff:
```python
import functools
import math

import jax
import jax.numpy as jnp
from jax import lax
from jax.experimental import pallas as pl
from jax.experimental.pallas import tpu as pltpu
from jax.sharding import Mesh
from jax.sharding import PartitionSpec as P

R = 12288
GATE = 64
TILE = 256
HALF = 32
FREQ = ("fx", "fc")
TILES = ("ty", "tz")
BF = jnp.bfloat16
F32 = jnp.float32


def make_table(freq_count, sample_count):
    freq_ids = lax.broadcasted_iota(jnp.int32, (freq_count, sample_count), 0)
    sample_ids = lax.broadcasted_iota(jnp.int32, (freq_count, sample_count), 1)
    phase_ids = freq_ids * sample_ids % sample_count
    angles = phase_ids.astype(F32) * (2.0 * math.pi / sample_count)
    amplitude = 1.0 / math.sqrt(GATE)
    return jnp.stack([jnp.cos(angles) * amplitude, -jnp.sin(angles) * amplitude]).astype(BF)


def params(mib=56):
    return pltpu.CompilerParams(vmem_limit_bytes=mib * 2**20)


def dft_kernel(starts_ref, tab_ref, plus_ref, minus_ref, out_ref):
    b = pl.program_id(0)
    lane = lax.broadcasted_iota(jnp.int32, (1, 256), 1)
    sample = lane & 127
    upper = lane >= 128
    row_source = lax.broadcasted_iota(jnp.int32, (256, 256), 0) & 15
    acc = [jnp.zeros((256, 256), F32), jnp.zeros((256, 256), F32)]
    for p in range(8):
        start = jnp.where(upper, starts_ref[2 * p + 1, b], starts_ref[2 * p, b])
        inside = (sample >= start) & (sample < start + GATE)
        source = jnp.where(inside, jnp.where(upper, 2 * p + 1, 2 * p), -1)
        table = jnp.where(row_source == source, tab_ref[...], 0.0).astype(BF)
        for q, ref in enumerate((plus_ref, minus_ref)):
            data = ref[2 * p : 2 * p + 2].reshape(256, 256)
            acc[q] += jnp.dot(table, data, preferred_element_type=F32)
    first = acc[0].reshape(8, 2, 16, 256)
    second = acc[1].reshape(8, 2, 16, 256)
    out_ref[:, 0, 0] = first[:, 0].astype(BF)
    out_ref[:, 1, 0] = first[:, 1].astype(BF)
    out_ref[:, 0, 1] = second[:, 0].astype(BF)
    out_ref[:, 1, 1] = (-second[:, 1]).astype(BF)


def dft(plus_time, minus_time, gate_starts, table):
    sources, samples, receivers = plus_time.shape
    blocks = receivers // TILE
    data = pl.BlockSpec((sources, samples, TILE), lambda b: (0, 0, b))
    return pl.pallas_call(
        dft_kernel,
        grid=(blocks,),
        in_specs=[
            pl.BlockSpec(memory_space=pltpu.SMEM),
            pl.BlockSpec((256, 256), lambda b: (0, 0)),
            data,
            data,
        ],
        out_specs=pl.BlockSpec((8, 2, 2, 16, TILE), lambda b: (0, 0, 0, 0, b)),
        out_shape=jax.ShapeDtypeStruct((8, 2, 2, 16, receivers), BF),
        compiler_params=params(),
        cost_estimate=pl.CostEstimate(
            flops=2 * 2 * 256 * 2048 * receivers, bytes_accessed=7 * 2**20, transcendentals=0
        ),
    )(gate_starts, table, plus_time, minus_time)


def fill_weights(w_ref, x_ref):
    for q in range(2):
        re = x_ref[:, 0, q].reshape(128, TILE).T
        im = x_ref[:, 1, q].reshape(128, TILE).T
        near, far = slice(q * 128, (q + 1) * 128), slice(256 + q * 128, 384 + q * 128)
        w_ref[0:256, near] = re
        w_ref[0:256, far] = im
        w_ref[256:512, near] = -im
        w_ref[256:512, far] = re


def coeff_kernel(ichunk, ranks_ref, x_ref, v_ref, out_ref, w_ref):
    j, ic = pl.program_id(0), pl.program_id(1)

    @pl.when(ic == 0)
    def _():
        fill_weights(w_ref, x_ref)

    prod = jnp.dot(
        v_ref[:, 0, 0].reshape(ichunk * HALF, TILE), w_ref[0:256], preferred_element_type=F32
    )
    prod += jnp.dot(
        v_ref[:, 0, 1].reshape(ichunk * HALF, TILE), w_ref[256:512], preferred_element_type=F32
    )
    rank_ids = lax.broadcasted_iota(jnp.int32, (HALF, 512), 0)
    for ii in range(ichunk):
        tile = prod[ii * HALF : (ii + 1) * HALF]
        kept = jnp.where(rank_ids < ranks_ref[ic * ichunk + ii, j], tile, 0.0)
        out_ref[ii // 3, ii % 3, 0] = kept.astype(BF)


def coefficients(spectra, v_factors, ranks):
    rows, cols = v_factors.shape[:2]
    ichunk = rows // 2
    return pl.pallas_call(
        functools.partial(coeff_kernel, ichunk),
        grid=(cols, rows // ichunk),
        in_specs=[
            pl.BlockSpec(memory_space=pltpu.SMEM),
            pl.BlockSpec((8, 2, 2, 16, TILE), lambda j, i: (0, 0, 0, 0, j)),
            pl.BlockSpec((ichunk, 1, 2, HALF, TILE), lambda j, i: (i, j, 0, 0, 0)),
        ],
        out_specs=pl.BlockSpec((ichunk // 3, 3, 1, HALF, 512), lambda j, i: (i, 0, j, 0, 0)),
        out_shape=jax.ShapeDtypeStruct((rows // 3, 3, cols, HALF, 512), BF),
        scratch_shapes=[pltpu.VMEM((512, 512), BF)],
        compiler_params=params(),
        cost_estimate=pl.CostEstimate(
            flops=2 * rows * cols * HALF * 512 * 512, bytes_accessed=10 * 2**20, transcendentals=0
        ),
    )(ranks, spectra, v_factors)


def band_kernel(place_ref, ranks_ref, x_ref, va_ref, vb_ref, vc_ref, band_ref, up_ref, down_ref, w_ref):
    jl = pl.program_id(0)
    last_row = ranks_ref.shape[0] - 1
    fill_weights(w_ref, x_ref)
    refs = (va_ref, vb_ref, vc_ref)
    prod = jnp.dot(
        jnp.concatenate([ref[0, 0, 0] for ref in refs], axis=0),
        w_ref[0:256],
        preferred_element_type=F32,
    )
    prod += jnp.dot(
        jnp.concatenate([ref[0, 0, 1] for ref in refs], axis=0),
        w_ref[256:512],
        preferred_element_type=F32,
    )
    rank_ids = lax.broadcasted_iota(jnp.int32, (HALF, 512), 0) + HALF
    kept = []
    for n in range(3):
        i = place_ref[0] * 3 + jl + n - 1
        rank = ranks_ref[jnp.clip(i, 0, last_row), jl]
        rank = jnp.where((i >= 0) & (i <= last_row), rank, 0)
        kept.append(jnp.where(rank_ids < rank, prod[n * HALF : (n + 1) * HALF], 0.0).astype(BF))

    @pl.when(jl == 0)
    def _():
        band_ref[...] = jnp.zeros_like(band_ref)
        up_ref[...] = kept[0]

    @pl.when(jl == 2)
    def _():
        down_ref[...] = kept[2]

    for n in range(3):
        il = jl + n - 1

        @pl.when((il >= 0) & (il < 3))
        def _():
            band_ref[il, 2 - n] = kept[n]


def band_coefficients(spectra, v_factors, ranks, place):
    rows = v_factors.shape[0]

    def spec(off):
        return pl.BlockSpec(
            (1, 1, 2, HALF, TILE),
            lambda j, place: (jnp.clip(place[0] * 3 + j + off, 0, rows - 1), j, 0, 1, 0),
        )

    edge = pl.BlockSpec((HALF, 512), lambda j, place: (0, 0))
    return pl.pallas_call(
        band_kernel,
        grid_spec=pltpu.PrefetchScalarGridSpec(
            num_scalar_prefetch=1,
            grid=(3,),
            in_specs=[
                pl.BlockSpec(memory_space=pltpu.SMEM),
                pl.BlockSpec((8, 2, 2, 16, TILE), lambda j, place: (0, 0, 0, 0, j)),
                spec(-1),
                spec(0),
                spec(1),
            ],
            out_specs=[
                pl.BlockSpec((3, 4, HALF, 512), lambda j, place: (0, 0, 0, 0)),
                edge,
                edge,
            ],
            scratch_shapes=[pltpu.VMEM((512, 512), BF)],
        ),
        out_shape=[
            jax.ShapeDtypeStruct((3, 4, HALF, 512), BF),
            jax.ShapeDtypeStruct((HALF, 512), BF),
            jax.ShapeDtypeStruct((HALF, 512), BF),
        ],
        compiler_params=params(),
        cost_estimate=pl.CostEstimate(
            flops=2 * 9 * HALF * 512 * 512, bytes_accessed=2 * 2**20, transcendentals=0
        ),
    )(place, ranks, spectra, v_factors, v_factors, v_factors)


def turn_kernel(chunks, place_ref, u_ref, ua_ref, ub_ref, uc_ref, low_ref, band_ref):
    g = pl.program_id(1)
    for c in range(2):
        for n in range(chunks):
            part = u_ref[0, n * 8 : (n + 1) * 8, c].reshape(256, TILE)
            low_ref[0, c, :, n * 256 : (n + 1) * 256] = part.T

    @pl.when(g == 0)
    def _():
        for c in range(2):
            parts = [r[0, 0, c] for r in (ua_ref, ub_ref, uc_ref)]
            part = jnp.concatenate([*parts, jnp.zeros_like(parts[0])], axis=0)
            band_ref[0, c] = part.T


def turned(u_factors, place):
    rows, all_cols = u_factors.shape[:2]

    def spec(off):
        return pl.BlockSpec(
            (1, 1, 2, HALF, TILE),
            lambda i, g, place: (i, jnp.clip(place[0] * 3 + i + off, 0, all_cols - 1), 0, 1, 0),
        )

    return pl.pallas_call(
        functools.partial(turn_kernel, 3),
        grid_spec=pltpu.PrefetchScalarGridSpec(
            num_scalar_prefetch=1,
            grid=(rows, 2),
            in_specs=[
                pl.BlockSpec((1, all_cols // 2, 2, HALF, TILE), lambda i, g, place: (i, g, 0, 0, 0)),
                spec(-1),
                spec(0),
                spec(1),
            ],
            out_specs=[
                pl.BlockSpec((1, 2, TILE, all_cols * HALF // 2), lambda i, g, place: (i, 0, 0, g)),
                pl.BlockSpec((1, 2, TILE, 128), lambda i, g, place: (i, 0, 0, 0)),
            ],
        ),
        out_shape=[
            jax.ShapeDtypeStruct((rows, 2, TILE, all_cols * HALF), BF),
            jax.ShapeDtypeStruct((rows, 2, TILE, 128), BF),
        ],
        compiler_params=params(),
        cost_estimate=pl.CostEstimate(flops=10**9, bytes_accessed=10 * 2**20, transcendentals=0),
    )(place, u_factors, u_factors, u_factors, u_factors)


def across(a, b):
    return lax.dot_general(a, b, (((1,), (1,)), ((), ())), preferred_element_type=F32)


def response_kernel(
    groups, c_ref, u_ref, band_ref, up_ref, down_ref, ub_ref,
    minus_ref, plus_ref, gram_ref, acc, gram_acc,
):
    i, g = pl.program_id(0), pl.program_id(1)
    sources, _, cols = c_ref.shape[:3]
    depth = sources * cols * HALF
    left = u_ref[0].reshape(512, depth)
    prod = jnp.dot(left, c_ref[:, 0].reshape(depth, 512), preferred_element_type=F32)

    @pl.when(g == 0)
    def _():
        acc[...] = prod

    @pl.when(g > 0)
    def _():
        acc[...] += prod

    @pl.when(g == groups - 1)
    def _():
        first = jnp.where(i == 0, up_ref[...], band_ref[0, 0])
        last = jnp.where(i == 2, down_ref[...], band_ref[0, 2])
        upper = jnp.concatenate([first, band_ref[0, 1], last, band_ref[0, 3]], axis=0)
        total = acc[...] + jnp.dot(ub_ref[0].reshape(512, 128), upper, preferred_element_type=F32)
        re = total[:256, :256] - total[256:, 256:]
        im = total[256:, :256] + total[:256, 256:]
        z_re = re.T.astype(BF)
        im = im.T
        z_im = jnp.concatenate([im[:128], -im[128:]], axis=0).astype(BF)
        p_re, p_im = z_re[128:], z_im[128:]
        minus_ref[0, 0] = z_re[:128]
        minus_ref[0, 1] = z_im[:128]
        plus_ref[0, 0] = p_re
        plus_ref[0, 1] = p_im
        g_re = across(z_re, p_re) + across(z_im, p_im)
        g_im = across(z_im, p_re) - across(z_re, p_im)

        @pl.when(i == 0)
        def _():
            gram_acc[0] = g_re
            gram_acc[1] = g_im

        @pl.when(i > 0)
        def _():
            gram_acc[0] += g_re
            gram_acc[1] += g_im

        @pl.when(i == 2)
        def _():
            for m, scale in enumerate((1.0 / math.sqrt(R), 1.0 / R)):
                for c in range(2):
                    part = gram_acc[c, m * 128 : (m + 1) * 128] * scale
                    gram_ref[:, m, c] = part.reshape(16, 8, 128)


def respond(coeffs, turned_low, turned_band, band, up, down):
    sources = coeffs.shape[0]
    rows = turned_low.shape[0]
    groups = 2
    per = sources // groups
    edge = pl.BlockSpec((HALF, 512), lambda i, g: (0, 0))
    field = pl.BlockSpec((1, 2, 128, TILE), lambda i, g: (0, 0, 0, i))
    return pl.pallas_call(
        functools.partial(response_kernel, groups),
        grid=(rows, groups),
        in_specs=[
            pl.BlockSpec((per, 1, 3, HALF, 512), lambda i, g: (g, i, 0, 0, 0)),
            pl.BlockSpec((1, 2, TILE, 3 * per * HALF), lambda i, g: (i, 0, 0, g)),
            pl.BlockSpec((1, 4, HALF, 512), lambda i, g: (i, 0, 0, 0)),
            edge,
            edge,
            pl.BlockSpec((1, 2, TILE, 128), lambda i, g: (i, 0, 0, 0)),
        ],
        out_specs=[
            field,
            field,
            pl.BlockSpec((16, 2, 2, 8, 128), lambda i, g: (0, 0, 0, 0, 0)),
        ],
        scratch_shapes=[pltpu.VMEM((512, 512), F32), pltpu.VMEM((2, 256, 128), F32)],
        out_shape=[
            jax.ShapeDtypeStruct((1, 2, 128, rows * TILE), BF),
            jax.ShapeDtypeStruct((1, 2, 128, rows * TILE), BF),
            jax.ShapeDtypeStruct((16, 2, 2, 8, 128), F32),
        ],
        compiler_params=params(),
        cost_estimate=pl.CostEstimate(
            flops=2 * 144 * HALF * 512 * 512, bytes_accessed=11 * 2**20, transcendentals=0
        ),
    )(coeffs, turned_low, band, up, down, turned_band)


def on_device(plus_time, minus_time, gate_starts, tile_ranks, u_factors, v_factors):
    u_factors, v_factors, ranks = u_factors[0], v_factors[0], tile_ranks[0]
    place = lax.axis_index(TILES).astype(jnp.int32).reshape(1)
    rows = make_table(8, 128).astype(F32).transpose(1, 0, 2)
    rows = jnp.broadcast_to(rows[:, :, None], (8, 2, 16, 128)).reshape(256, 128)
    table = jnp.concatenate([rows, rows], axis=1)
    local_spec = dft(plus_time, minus_time, gate_starts, table)
    spectra = lax.all_to_all(local_spec, FREQ, 0, 0, tiled=True)
    band, up, down = band_coefficients(spectra, v_factors, ranks, place)
    size = lax.axis_size(TILES)
    from_below = lax.ppermute(down, TILES, [(i, i + 1) for i in range(size - 1)])
    from_above = lax.ppermute(up, TILES, [(i + 1, i) for i in range(size - 1)])
    spectra, band = lax.optimization_barrier((spectra, band))
    coeffs = coefficients(spectra, v_factors, ranks)
    coeffs, from_below, from_above = lax.optimization_barrier((coeffs, from_below, from_above))
    arrived = lax.all_to_all(coeffs, TILES, 0, 0, tiled=True)
    low, low_band = turned(u_factors, place)
    minus_new, plus_new, gram = respond(arrived, low, low_band, band, from_below, from_above)
    sums = lax.all_to_all(gram, TILES, 0, 0, tiled=True).sum(axis=0)
    return (minus_new, plus_new, sums[None, 0], sums[None, 1])


def solution(mesh):
    torus = Mesh(mesh.devices.reshape(4, 2, 4, 4), (*FREQ, *TILES))
    in_specs = (
        P(FREQ, None, TILES),
        P(FREQ, None, TILES),
        P(FREQ, TILES),
        P(FREQ, None, TILES),
        P(FREQ, TILES, None, None, None, None),
        P(FREQ, None, TILES, None, None, None),
    )
    out_specs = (
        P(FREQ, None, None, TILES),
        P(FREQ, None, None, TILES),
        P(FREQ, None, TILES, None),
        P(FREQ, None, TILES, None),
    )
    return jax.shard_map(
        on_device, mesh=torus, in_specs=in_specs, out_specs=out_specs, check_vma=False
    )
```

time: 176 us -> 149 us (0.85)
  local copies, waits for them, and re-layouts: 47.1 us -> 4.18 us
  waiting for transfers between devices: 32.7 us -> 67.7 us
  Pallas kernels: 0 us -> 34.6 us
  other arithmetic: 28.9 us -> 0.81 us
  matrix products: 22 us -> 0 us
  blocking collectives: 24.8 us -> 20.4 us
    all_to_all x2, waiting for transfers between devices: 32.7 us -> 67.7 us  [the longest x1 55.2 us: on_device(): arrived = lax.all_to_all(coeffs, TILES, 0, 0, tiled=True)]
    pallas_call x0 -> x5, Pallas kernels: none -> 34.6 us  [the longest x1 10.4 us: respond(): pl.pallas_call(functools.partial(response_kernel, groups), grid=(rows, gr...]
    gather x6 -> x0, local copies, waits for them, and re-layouts: 25.5 us -> none  [the longest x3 12.7 us: on_device(): u_band.append(u_factors[:, row_local, partner][:, :, :, half_depth:])]
    another operation x11 -> x1, other arithmetic: 24.5 us -> 0.05 us  [the longest x3 21.9 us: on_device(): jnp.stack([coeff_real * rank_mask, coeff_imag * rank_mask], 3)]
    dot_general x5 -> x0, matrix products: 22 us -> none  [the longest x1 17.3 us: on_device(): jnp.einsum('fijckr,fdsjr->fijcdks', v_factors, columns, preferred_element...]
    all_to_all x4 -> x0, local copies, waits for them, and re-layouts: 5.43 us -> none  [the longest x2 3.62 us: on_device(): lax.all_to_all(lower_part, 'tile', split_axis=1, concat_axis=2, tiled=True)]
    all_to_all x2 -> x1, blocking collectives: 24.8 us -> 20.4 us  [on_device(): sums = lax.all_to_all(gram, TILES, 0, 0, tiled=True).sum(axis=0)]
    squeeze x5 -> x0, local copies, waits for them, and re-layouts: 3.49 us -> none  [the longest x2 2.36 us: on_device(): resp_real = products[:, 0, 0] - sign_vec[:, None, None] * products[:, 1, 1]]
  transfers between devices with their start and end apart: 4 -> 4, of which waited for: 2 -> 2; matrix products, arithmetic and copies ran while one was open for 23% -> 0% of each run, Pallas kernels for 0% -> 10%
where the time goes in v1:
time: 149 us; the launch traced here: 147 us
  waiting for transfers between devices  67.7 us (45%)
  Pallas kernels  34.6 us (23%)
  blocking collectives  20.4 us (14%)
  starting transfers between devices  18.3 us (12%)
  local copies, waits for them, and re-layouts  4.18 us (3%)
    all_to_all x1, waiting for transfers between devices, on_device(): arrived = lax.all_to_all(coeffs, TILES, 0, 0, tiled=True)  55.2 us
    all_to_all x1, blocking collectives, on_device(): sums = lax.all_to_all(gram, TILES, 0, 0, tiled=True).sum(axis=0)  20.4 us
    all_to_all x1, waiting for transfers between devices, on_device(): spectra = lax.all_to_all(local_spec, FREQ, 0, 0, tiled=True)  12.4 us
    pallas_call x1, Pallas kernels, respond(): pl.pallas_call(functools.partial(response_kernel, groups), grid=(rows, gr...  10.4 us
    all_to_all x1, starting transfers between devices, on_device(): arrived = lax.all_to_all(coeffs, TILES, 0, 0, tiled=True)  8.82 us
    pallas_call x1, Pallas kernels, coefficients(): pl.pallas_call(functools.partial(coeff_kernel, ichunk), grid=(cols, rows...  8.02 us
    pallas_call x1, Pallas kernels, turned(): pl.pallas_call(functools.partial(turn_kernel, 3), grid_spec=pltpu.Prefetc...  7.05 us
    pallas_call x1, Pallas kernels, dft(): pl.pallas_call(dft_kernel, grid=(blocks,), in_specs=[pl.BlockSpec(memory_...  5.46 us
  transfers between devices with their start and end apart: 4, of which 2 were waited for; matrix products, arithmetic and copies ran while one was open for 0% of the time, Pallas kernels for 10%

profile of v1, /device:TPU:0, one launch (start us, length us, event | category | flops | bytes accessed | tf_op | source)
XLA Modules:
  0.0 146.7 jit_solution(458276465403410346)
XLA Ops:
  0.6 0.1 multiply_convert_fusion
  0.7 1.4 copy.14.starts_ref
  2.1 0.0 copy-start.3
  2.1 0.7 pad_maximum_fusion.tab_ref
  2.8 5.5 %shard_map.93 = bf16[8,2,2,16,768]{4,3,2,1,0:T(8,128)(2,1)} custom-call(s32[16,3]{1,0:T(8,128)} %copy.14.starts_ref, f32[256,256]{1,0:T(8,128)} %pad_maximum_fusion.tab_ref, bf16[16,128,768]{2,1,0:T(8,128)(2,1)} %plus_ref.1, bf16[16,128,768]{2,1,0:T(8,128)(2,1)} %minus_ref.1), custom_call_target="tpu_custom_call" | custom-call | flops 1610612736 | bytes 7340032 | tf_op jit(solution)/shard_map/pallas_call | solution.py:62
  8.3 4.4 %all-to-all-start = ((bf16[8,2,2,16,768]{4,3,2,1,0:T(8,128)(2,1)}), bf16[8,2,2,16,768]{4,3,2,1,0:T(8,128)(2,1)S(1)}, u32[]{:S(2)}, u32[]{:S(2)}) async-start(bf16[8,2,2,16,768]{4,3,2,1,0:T(8,128)(2,1)} %shard_map.93), calls=%async_computation | async-start | bytes 1572864 | tf_op jit(solution)/shard_map/all_to_all | solution.py:364
  12.6 0.0 copy-done.3
  12.7 0.7 copy.12
  13.4 12.4 %all-to-all-done.x_ref = bf16[8,2,2,16,768]{4,3,2,1,0:T(8,128)(2,1)S(1)} async-done(((bf16[8,2,2,16,768]{4,3,2,1,0:T(8,128)(2,1)}), bf16[8,2,2,16,768]{4,3,2,1,0:T(8,128)(2,1)S(1)}, u32[]{:S(2)}, u32[]{:S(2)}) %all-to-all-start) | async-done | bytes 786464 | tf_op jit(solution)/shard_map/all_to_all | solution.py:364
  25.8 0.0 copy-start
  25.8 0.9 copy-done
  26.7 3.7 %shard_map.94 = (bf16[3,4,32,512]{3,2,1,0:T(8,128)(2,1)}, bf16[32,512]{1,0:T(8,128)(2,1)}, bf16[32,512]{1,0:T(8,128)(2,1)}) custom-call(s32[1]{0:T(128)} %bitcast.3.place_ref, s32[48,3]{1,0:T(8,128)} %bitcast.16, bf16[8,2,2,16,768]{4,3,2,1,0:T(8,128)(2,1)} %copy-done, bf16[48,3,2,64,256]{4,3,2,1,0:T(8,128)(2,1)} %bitcast.11, ...), custom_call_target="tpu_custom_call" | custom-call | flops 150994944 | bytes 2097152 | tf_op jit(solution)/shard_map/pallas_call | solution.py:182
  30.4 3.8 %collective-permute-start = (bf16[32,512]{1,0:T(8,128)(2,1)}, bf16[32,512]{1,0:T(8,128)(2,1)S(1)}, u32[]{:S(2)}, u32[]{:S(2)}) collective-permute-start(bf16[32,512]{1,0:T(8,128)(2,1)} %get-tuple-element.19), channel_id=1, source_target_pairs={{0,1},{1,2},{2,3},{3,4},{4,5},{5,6},{6,7},{7,8},{8,9},{9,10},{10,1... | collective-permute-start | bytes 98312 | tf_op jit(solution)/shard_map/ppermute | solution.py:367
  34.2 1.3 collective-permute-start.1
  35.5 8.0 %shard_map.95 = bf16[16,3,3,32,512]{4,3,2,1,0:T(8,128)(2,1)} custom-call(s32[48,3]{1,0:T(8,128)} %bitcast.17, bf16[8,2,2,16,768]{4,3,2,1,0:T(8,128)(2,1)} %copy-done, bf16[48,3,2,64,256]{4,3,2,1,0:T(8,128)(2,1)} %bitcast.14), custom_call_target="tpu_custom_call" | custom-call | flops 2415919104 | bytes 10485760 | tf_op jit(solution)/shard_map/pallas_call | solution.py:114
  43.5 0.0 collective-permute-done.up_ref
  43.5 0.0 copy-start.1
  43.5 0.0 collective-permute-done.1.down_ref
  43.5 0.0 copy-start.2
  43.6 0.6 copy-done.1
  44.1 0.0 copy-done.2
  44.2 8.8 %all-to-all-start.1 = ((bf16[16,3,3,32,512]{4,3,2,1,0:T(8,128)(2,1)}), bf16[16,3,3,32,512]{4,3,2,1,0:T(8,128)(2,1)}, u32[]{:S(2)}, u32[]{:S(2)}) async-start(bf16[16,3,3,32,512]{4,3,2,1,0:T(8,128)(2,1)} %shard_map.95), calls=%async_computation.1 | async-start | bytes 9437184 | tf_op jit(solution)/shard_map/all_to_all | solution.py:372
  53.0 7.0 %shard_map.96 = (bf16[3,2,256,1536]{3,2,1,0:T(8,128)(2,1)}, bf16[3,2,256,128]{3,2,1,0:T(8,128)(2,1)}) custom-call(s32[1]{0:T(128)} %bitcast.3.place_ref, bf16[3,48,2,64,256]{4,3,2,1,0:T(8,128)(2,1)} %bitcast.7, bf16[3,48,2,64,256]{4,3,2,1,0:T(8,128)(2,1)} %bitcast.8, bf16[3,48,2,64,256]{4,3,2,1,0:T(8,128)(2,1)} %bitcast.9, bf16[3,48,2,64,256]{4,3,2,1,0:T(8,128)(2,1)} %bitcast.10), custom_call_target="tpu_custom_call" | custom-call | flops 1000000000 | bytes 10485760 | tf_op jit(solution)/shard_map/pallas_call | solution.py:237
  60.0 55.2 %all-to-all-done.1.c_ref = bf16[16,3,3,32,512]{4,3,2,1,0:T(8,128)(2,1)} async-done(((bf16[16,3,3,32,512]{4,3,2,1,0:T(8,128)(2,1)}), bf16[16,3,3,32,512]{4,3,2,1,0:T(8,128)(2,1)}, u32[]{:S(2)}, u32[]{:S(2)}) %all-to-all-start.1) | async-done | bytes 4718624 | tf_op jit(solution)/shard_map/all_to_all | solution.py:372
  115.3 10.4 %shard_map.97 = (bf16[1,2,128,768]{3,2,1,0:T(8,128)(2,1)}, bf16[1,2,128,768]{3,2,1,0:T(8,128)(2,1)}, f32[16,2,2,8,128]{4,3,2,1,0:T(8,128)}) custom-call(bf16[16,3,3,32,512]{4,3,2,1,0:T(8,128)(2,1)} %all-to-all-done.1.c_ref, bf16[3,2,256,1536]{3,2,1,0:T(8,128)(2,1)} %get-tuple-element.22.u_ref, bf16[3,4,32,512]{3,2,1,0:T(8,128)(2,1)} %get-tuple-element.23.band_ref, ...), custom_call_target="tpu_custom_call" | custom-call | flops 2415919104 | bytes 11534336 | tf_op jit(solution)/shard_map/pallas_call | solution.py:328
  125.7 20.4 %all_to_all.15 = f32[16,2,2,8,128]{4,3,2,1,0:T(8,128)S(1)} all-to-all(f32[16,2,2,8,128]{4,3,2,1,0:T(8,128)} %get-tuple-element.29), channel_id=1, replica_groups=mesh['fx'=4,'fc'=2,'ty'=4,'tz'=4] {'ty','tz'}, dimensions={0} | all-to-all | bytes 524288 | tf_op jit(solution)/shard_map/all_to_all | solution.py:375
  146.1 0.6 fusion.6
  (4 shorter events, 0.0 us)
Async XLA Ops:
  2.1 10.6 %copy-start.3 = (s32[1,48,3]{1,0,2:T(1,128)S(1)}, s32[1,48,3]{1,0,2:T(1,128)}, u32[]{:S(2)}) copy-start(s32[1,48,3]{1,0,2:T(1,128)} %param.9) | copy-start | bytes 1732
  8.3 17.5 %all-to-all-start = ((bf16[8,2,2,16,768]{4,3,2,1,0:T(8,128)(2,1)}), bf16[8,2,2,16,768]{4,3,2,1,0:T(8,128)(2,1)S(1)}, u32[]{:S(2)}, u32[]{:S(2)}) async-start(bf16[8,2,2,16,768]{4,3,2,1,0:T(8,128)(2,1)} %shard_map.93), calls=%async_computation | async-start | bytes 1572864 | tf_op jit(solution)/shard_map/all_to_all | solution.py:364
  25.8 0.9 copy-start
  30.4 13.1 %collective-permute-start = (bf16[32,512]{1,0:T(8,128)(2,1)}, bf16[32,512]{1,0:T(8,128)(2,1)S(1)}, u32[]{:S(2)}, u32[]{:S(2)}) collective-permute-start(bf16[32,512]{1,0:T(8,128)(2,1)} %get-tuple-element.19), channel_id=1, source_target_pairs={{0,1},{1,2},{2,3},{3,4},{4,5},{5,6},{6,7},{7,8},{8,9},{9,10},{10,1... | collective-permute-start | bytes 98312 | tf_op jit(solution)/shard_map/ppermute | solution.py:367
  34.2 9.3 %collective-permute-start.1 = (bf16[32,512]{1,0:T(8,128)(2,1)}, bf16[32,512]{1,0:T(8,128)(2,1)S(1)}, u32[]{:S(2)}, u32[]{:S(2)}) collective-permute-start(bf16[32,512]{1,0:T(8,128)(2,1)} %get-tuple-element.20), channel_id=1, source_target_pairs={{1,0},{2,1},{3,2},{4,3},{5,4},{6,5},{7,6},{8,7},{9,8},{10,9},{11,1... | collective-permute-start | bytes 98312 | tf_op jit(solution)/shard_map/ppermute | solution.py:368
  43.5 0.6 copy-start.1
  43.5 0.6 copy-start.2
  44.2 71.1 %all-to-all-start.1 = ((bf16[16,3,3,32,512]{4,3,2,1,0:T(8,128)(2,1)}), bf16[16,3,3,32,512]{4,3,2,1,0:T(8,128)(2,1)}, u32[]{:S(2)}, u32[]{:S(2)}) async-start(bf16[16,3,3,32,512]{4,3,2,1,0:T(8,128)(2,1)} %shard_map.95), calls=%async_computation.1 | async-start | bytes 9437184 | tf_op jit(solution)/shard_map/all_to_all | solution.py:372

commit v2 on v1

v2 whole, which is shorter than its diff:
```python
import functools
import math

import jax
import jax.numpy as jnp
from jax import lax
from jax.experimental import pallas as pl
from jax.experimental.pallas import tpu as pltpu
from jax.sharding import Mesh
from jax.sharding import PartitionSpec as P

R = 12288
GATE = 64
TILE = 256
HALF = 32
FREQ = ("fx", "fc")
TILES = ("ty", "tz")
BF = jnp.bfloat16
F32 = jnp.float32


def make_table(freq_count, sample_count):
    freq_ids = lax.broadcasted_iota(jnp.int32, (freq_count, sample_count), 0)
    sample_ids = lax.broadcasted_iota(jnp.int32, (freq_count, sample_count), 1)
    phase_ids = freq_ids * sample_ids % sample_count
    angles = phase_ids.astype(F32) * (2.0 * math.pi / sample_count)
    amplitude = 1.0 / math.sqrt(GATE)
    return jnp.stack([jnp.cos(angles) * amplitude, -jnp.sin(angles) * amplitude]).astype(BF)


def params(mib=56):
    return pltpu.CompilerParams(vmem_limit_bytes=mib * 2**20)


def dft_kernel(starts_ref, tab_ref, plus_hbm, minus_hbm, out_ref, t_ref, data_ref, sems):
    copies = []
    for b in range(3):
        for q, ref in enumerate((plus_hbm, minus_hbm)):
            src = ref.at[:, :, pl.ds(b * TILE, TILE)]
            copies.append(pltpu.make_async_copy(src, data_ref.at[b, q], sems.at[b, q]))
            copies[-1].start()
    lane = lax.broadcasted_iota(jnp.int32, (1, 256), 1)
    sample = lane & 127
    upper = lane >= 128
    row_source = lax.broadcasted_iota(jnp.int32, (256, 256), 0) & 15
    for b in range(3):
        for p in range(8):
            start = jnp.where(upper, starts_ref[b, 2 * p + 1], starts_ref[b, 2 * p])
            inside = (sample >= start) & (sample < start + GATE)
            source = jnp.where(inside, jnp.where(upper, 2 * p + 1, 2 * p), -1)
            table = jnp.where(row_source == source, tab_ref[...], 0.0).astype(BF)
            t_ref[b % 2, :, p * 256 : (p + 1) * 256] = table
        for q in range(2):
            copies[2 * b + q].wait()
            data = data_ref[b, q].reshape(2048, 256)
            prod = jnp.dot(t_ref[b % 2], data, preferred_element_type=F32)
            prod = prod.reshape(8, 2, 16, 256)
            lanes = slice(b * TILE, (b + 1) * TILE)
            out_ref[:, 0, q, :, lanes] = prod[:, 0].astype(BF)
            out_ref[:, 1, q, :, lanes] = (prod[:, 1] if q == 0 else -prod[:, 1]).astype(BF)


def dft(plus_time, minus_time, gate_starts, table):
    sources, samples, receivers = plus_time.shape
    return pl.pallas_call(
        dft_kernel,
        in_specs=[
            pl.BlockSpec(memory_space=pltpu.SMEM),
            pl.BlockSpec(memory_space=pltpu.VMEM),
            pl.BlockSpec(memory_space=pl.ANY),
            pl.BlockSpec(memory_space=pl.ANY),
        ],
        out_specs=pl.BlockSpec(memory_space=pltpu.VMEM),
        out_shape=jax.ShapeDtypeStruct((8, 2, 2, 16, receivers), BF),
        scratch_shapes=[
            pltpu.VMEM((2, 256, 2048), BF),
            pltpu.VMEM((3, 2, sources, samples, TILE), BF),
            pltpu.SemaphoreType.DMA((3, 2)),
        ],
        compiler_params=params(),
        cost_estimate=pl.CostEstimate(
            flops=2 * 2 * 256 * 2048 * receivers, bytes_accessed=7 * 2**20, transcendentals=0
        ),
    )(gate_starts, table, plus_time, minus_time)


def fill_weights(w_ref, x_ref):
    for q in range(2):
        re = x_ref[:, 0, q].reshape(128, TILE).T
        im = x_ref[:, 1, q].reshape(128, TILE).T
        near, far = slice(q * 128, (q + 1) * 128), slice(256 + q * 128, 384 + q * 128)
        w_ref[0:256, near] = re
        w_ref[0:256, far] = im
        w_ref[256:512, near] = -im
        w_ref[256:512, far] = re


def coeff_kernel(ranks_ref, x_ref, v_hbm, out_hbm, v_ref, o_ref, w_ref, sems):
    arrivals, sends = [], []
    for j in range(3):
        src = v_hbm.at[:, j, :, pl.ds(0, HALF), :]
        arrivals.append(pltpu.make_async_copy(src, v_ref.at[j], sems.at[0, j]))
        arrivals[-1].start()
    rank_ids = lax.broadcasted_iota(jnp.int32, (HALF, 512), 0)
    for j in range(3):
        fill_weights(w_ref, x_ref.at[:, :, :, :, pl.ds(j * TILE, TILE)])
        arrivals[j].wait()
        for h in range(4):
            rows = slice(h * 12, (h + 1) * 12)
            v = jnp.concatenate([v_ref[j, rows, c].reshape(12 * HALF, TILE) for c in range(2)], axis=1)
            prod = jnp.dot(v, w_ref[...], preferred_element_type=F32)
            for n in range(12):
                i = h * 12 + n
                kept = jnp.where(rank_ids < ranks_ref[j, i], prod[n * HALF : (n + 1) * HALF], 0.0)
                o_ref[j, i // 3, i % 3] = kept.astype(BF)
        sends.append(pltpu.make_async_copy(o_ref.at[j], out_hbm.at[:, :, j], sems.at[1, j]))
        sends[-1].start()
    for send in sends:
        send.wait()


def coefficients(spectra, v_factors, ranks):
    rows, cols = v_factors.shape[:2]
    return pl.pallas_call(
        coeff_kernel,
        in_specs=[
            pl.BlockSpec(memory_space=pltpu.SMEM),
            pl.BlockSpec(memory_space=pltpu.VMEM),
            pl.BlockSpec(memory_space=pl.ANY),
        ],
        out_specs=pl.BlockSpec(memory_space=pl.ANY),
        out_shape=jax.ShapeDtypeStruct((rows // 3, 3, cols, HALF, 512), BF),
        scratch_shapes=[
            pltpu.VMEM((cols, rows, 2, HALF, TILE), BF),
            pltpu.VMEM((cols, rows // 3, 3, HALF, 512), BF),
            pltpu.VMEM((512, 512), BF),
            pltpu.SemaphoreType.DMA((2, 3)),
        ],
        compiler_params=params(),
        cost_estimate=pl.CostEstimate(
            flops=2 * rows * cols * HALF * 512 * 512, bytes_accessed=10 * 2**20, transcendentals=0
        ),
    )(ranks, spectra, v_factors)


def band_kernel(place_ref, ranks_ref, x_ref, va_ref, vb_ref, vc_ref, band_ref, up_ref, down_ref, w_ref):
    jl = pl.program_id(0)
    last_row = ranks_ref.shape[1] - 1
    fill_weights(w_ref, x_ref)
    refs = (va_ref, vb_ref, vc_ref)
    prod = jnp.dot(
        jnp.concatenate([ref[0, 0, 0] for ref in refs], axis=0),
        w_ref[0:256],
        preferred_element_type=F32,
    )
    prod += jnp.dot(
        jnp.concatenate([ref[0, 0, 1] for ref in refs], axis=0),
        w_ref[256:512],
        preferred_element_type=F32,
    )
    rank_ids = lax.broadcasted_iota(jnp.int32, (HALF, 512), 0) + HALF
    kept = []
    for n in range(3):
        i = place_ref[0] * 3 + jl + n - 1
        rank = ranks_ref[jl, jnp.clip(i, 0, last_row)]
        rank = jnp.where((i >= 0) & (i <= last_row), rank, 0)
        kept.append(jnp.where(rank_ids < rank, prod[n * HALF : (n + 1) * HALF], 0.0).astype(BF))

    @pl.when(jl == 0)
    def _():
        band_ref[...] = jnp.zeros_like(band_ref)
        up_ref[...] = kept[0]

    @pl.when(jl == 2)
    def _():
        down_ref[...] = kept[2]

    for n in range(3):
        il = jl + n - 1

        @pl.when((il >= 0) & (il < 3))
        def _():
            band_ref[il, 2 - n] = kept[n]


def band_coefficients(spectra, v_factors, ranks, place):
    rows = v_factors.shape[0]

    def spec(off):
        return pl.BlockSpec(
            (1, 1, 2, HALF, TILE),
            lambda j, place: (jnp.clip(place[0] * 3 + j + off, 0, rows - 1), j, 0, 1, 0),
        )

    edge = pl.BlockSpec((HALF, 512), lambda j, place: (0, 0))
    return pl.pallas_call(
        band_kernel,
        grid_spec=pltpu.PrefetchScalarGridSpec(
            num_scalar_prefetch=1,
            grid=(3,),
            in_specs=[
                pl.BlockSpec(memory_space=pltpu.SMEM),
                pl.BlockSpec((8, 2, 2, 16, TILE), lambda j, place: (0, 0, 0, 0, j)),
                spec(-1),
                spec(0),
                spec(1),
            ],
            out_specs=[
                pl.BlockSpec((3, 3, HALF, 512), lambda j, place: (0, 0, 0, 0)),
                edge,
                edge,
            ],
            scratch_shapes=[pltpu.VMEM((512, 512), BF)],
        ),
        out_shape=[
            jax.ShapeDtypeStruct((3, 3, HALF, 512), BF),
            jax.ShapeDtypeStruct((HALF, 512), BF),
            jax.ShapeDtypeStruct((HALF, 512), BF),
        ],
        compiler_params=params(),
        cost_estimate=pl.CostEstimate(
            flops=2 * 9 * HALF * 512 * 512, bytes_accessed=2 * 2**20, transcendentals=0
        ),
    )(place, ranks, spectra, v_factors, v_factors, v_factors)


def response_kernel(
    place_ref, c_hbm, u_hbm, band_ref, up_ref, down_ref, minus_ref, plus_ref, gram_ref,
    c_ref, u_ref, b_ref, acc, sems,
):
    all_cols = u_hbm.shape[1]
    arrivals = []
    for i in range(3):
        low = pl.ds(0, HALF)
        pairs = [(c_hbm.at[:, i], c_ref.at[i]), (u_hbm.at[i, :, :, low, :], u_ref.at[i])]
        for n in range(3):
            col = jnp.clip(place_ref[0] * 3 + i + n - 1, 0, all_cols - 1)
            pairs.append((u_hbm.at[i, col, :, pl.ds(HALF, HALF), :], b_ref.at[i, n]))
        arrivals.append(
            [pltpu.make_async_copy(s, d, sems.at[i, k]) for k, (s, d) in enumerate(pairs)]
        )
        for copy in arrivals[-1]:
            copy.start()

    def product(c, u):
        right = jnp.concatenate(u, axis=1)
        return lax.dot_general(c, right, (((0,), (0,)), ((), ())), preferred_element_type=F32)

    for i in range(3):
        for copy in arrivals[i]:
            copy.wait()
        upper = [band_ref[i, n] for n in range(3)]
        if i == 0:
            upper[0] = up_ref[...]
        if i == 2:
            upper[2] = down_ref[...]
        prod = product(
            jnp.concatenate(upper, axis=0), [b_ref[i, :, c].reshape(3 * HALF, TILE) for c in range(2)]
        )
        prod += product(
            c_ref[i].reshape(all_cols * HALF, 512),
            [u_ref[i, :, c].reshape(all_cols * HALF, TILE) for c in range(2)],
        )
        re = (prod[:256, :256] - prod[256:, 256:]).astype(BF)
        im = prod[256:, :256] + prod[:256, 256:]
        im = jnp.concatenate([im[:128], -im[128:]], axis=0).astype(BF)
        lanes = slice(i * TILE, (i + 1) * TILE)
        minus_ref[0, 0, :, lanes] = re[:128]
        minus_ref[0, 1, :, lanes] = im[:128]
        plus_ref[0, 0, :, lanes] = re[128:]
        plus_ref[0, 1, :, lanes] = im[128:]
        gram = lax.dot_general(
            jnp.concatenate([re, im], axis=0),
            jnp.concatenate([re[128:], im[128:]], axis=0),
            (((1,), (1,)), ((), ())),
            preferred_element_type=F32,
        )
        if i == 0:
            acc[...] = gram
        else:
            acc[...] += gram
    gram = acc[...]
    parts = (gram[:256, :128] + gram[256:, 128:], gram[256:, :128] - gram[:256, 128:])
    for m, scale in enumerate((1.0 / math.sqrt(R), 1.0 / R)):
        for c, part in enumerate(parts):
            gram_ref[:, m, c] = (part[m * 128 : (m + 1) * 128] * scale).reshape(16, 8, 128)


def respond(coeffs, u_factors, band, up, down, place):
    rows, all_cols = u_factors.shape[:2]
    whole = pl.BlockSpec(memory_space=pltpu.VMEM)
    return pl.pallas_call(
        response_kernel,
        in_specs=[
            pl.BlockSpec(memory_space=pltpu.SMEM),
            pl.BlockSpec(memory_space=pl.ANY),
            pl.BlockSpec(memory_space=pl.ANY),
            whole,
            whole,
            whole,
        ],
        out_specs=[whole, whole, whole],
        scratch_shapes=[
            pltpu.VMEM((rows, all_cols // 3, 3, HALF, 512), BF),
            pltpu.VMEM((rows, all_cols, 2, HALF, TILE), BF),
            pltpu.VMEM((rows, 3, 2, HALF, TILE), BF),
            pltpu.VMEM((512, TILE), F32),
            pltpu.SemaphoreType.DMA((3, 5)),
        ],
        out_shape=[
            jax.ShapeDtypeStruct((1, 2, 128, rows * TILE), BF),
            jax.ShapeDtypeStruct((1, 2, 128, rows * TILE), BF),
            jax.ShapeDtypeStruct((16, 2, 2, 8, 128), F32),
        ],
        compiler_params=params(),
        cost_estimate=pl.CostEstimate(
            flops=2 * 144 * HALF * 512 * 512, bytes_accessed=11 * 2**20, transcendentals=0
        ),
    )(place, coeffs, u_factors, band, up, down)


def on_device(plus_time, minus_time, gate_starts, tile_ranks, u_factors, v_factors):
    u_factors, v_factors, ranks = u_factors[0], v_factors[0], tile_ranks[0].T
    place = lax.axis_index(TILES).astype(jnp.int32).reshape(1)
    rows = make_table(8, 128).astype(F32).transpose(1, 0, 2)
    rows = jnp.broadcast_to(rows[:, :, None], (8, 2, 16, 128)).reshape(256, 128)
    table = jnp.concatenate([rows, rows], axis=1)
    local_spec = dft(plus_time, minus_time, gate_starts.T, table)
    spectra = lax.all_to_all(local_spec, FREQ, 0, 0, tiled=True)
    band, up, down = band_coefficients(spectra, v_factors, ranks, place)
    size = lax.axis_size(TILES)
    from_below = lax.ppermute(down, TILES, [(i, i + 1) for i in range(size - 1)])
    from_above = lax.ppermute(up, TILES, [(i + 1, i) for i in range(size - 1)])
    spectra, band = lax.optimization_barrier((spectra, band))
    coeffs = coefficients(spectra, v_factors, ranks)
    coeffs, from_below, from_above = lax.optimization_barrier((coeffs, from_below, from_above))
    arrived = lax.all_to_all(coeffs, TILES, 0, 0, tiled=True)
    minus_new, plus_new, gram = respond(arrived, u_factors, band, from_below, from_above, place)
    sums = lax.all_to_all(gram, TILES, 0, 0, tiled=True).sum(axis=0)
    return (minus_new, plus_new, sums[None, 0], sums[None, 1])


def solution(mesh):
    torus = Mesh(mesh.devices.reshape(4, 2, 4, 4), (*FREQ, *TILES))
    in_specs = (
        P(FREQ, None, TILES),
        P(FREQ, None, TILES),
        P(FREQ, TILES),
        P(FREQ, None, TILES),
        P(FREQ, TILES, None, None, None, None),
        P(FREQ, None, TILES, None, None, None),
    )
    out_specs = (
        P(FREQ, None, None, TILES),
        P(FREQ, None, None, TILES),
        P(FREQ, None, TILES, None),
        P(FREQ, None, TILES, None),
    )
    return jax.shard_map(
        on_device, mesh=torus, in_specs=in_specs, out_specs=out_specs, check_vma=False
    )
```

time: 149 us -> 130 us (0.87); the launches traced: 147 us -> 130 us
  blocking collectives: 20.4 us -> 76.5 us
  waiting for transfers between devices: 67.7 us -> 12.6 us
  starting transfers between devices: 18.3 us -> 9.5 us
  Pallas kernels: 34.6 us -> 27.4 us
  local copies, waits for them, and re-layouts: 4.18 us -> 2.1 us
    all_to_all x0 -> x1, blocking collectives: none -> 64.6 us  [on_device(): arrived = lax.all_to_all(coeffs, TILES, 0, 0, tiled=True)]
    all_to_all x1 -> x0, waiting for transfers between devices: 55.2 us -> none  [on_device(): arrived = lax.all_to_all(coeffs, TILES, 0, 0, tiled=True)]
    all_to_all x1 -> x0, starting transfers between devices: 8.82 us -> none  [on_device(): arrived = lax.all_to_all(coeffs, TILES, 0, 0, tiled=True)]
    all_to_all x1, blocking collectives: 20.4 us -> 12 us  [on_device(): sums = lax.all_to_all(gram, TILES, 0, 0, tiled=True).sum(axis=0)]
    pallas_call x4 -> x3, Pallas kernels: 30.9 us -> 24 us  [the longest x1 9.93 us: respond(): pl.pallas_call(response_kernel, in_specs=[pl.BlockSpec(memory_space=pltpu...]
    unnamed x10 -> x9, local copies, waits for them, and re-layouts: 3.56 us -> 1.48 us
  transfers between devices with their start and end apart: 4 -> 3, of which waited for: 2 -> 1; matrix products, arithmetic and copies ran while one was open for 0% -> 0% of each run, Pallas kernels for 10% -> 5%
where the time goes in v2:
time: 130 us
  blocking collectives  76.5 us (59%)
  Pallas kernels  27.4 us (21%)
  waiting for transfers between devices  12.6 us (10%)
  starting transfers between devices  9.5 us (7%)
  local copies, waits for them, and re-layouts  2.1 us (2%)
    all_to_all x1, blocking collectives, on_device(): arrived = lax.all_to_all(coeffs, TILES, 0, 0, tiled=True)  64.6 us
    all_to_all x1, waiting for transfers between devices, on_device(): spectra = lax.all_to_all(local_spec, FREQ, 0, 0, tiled=True)  12.6 us
    all_to_all x1, blocking collectives, on_device(): sums = lax.all_to_all(gram, TILES, 0, 0, tiled=True).sum(axis=0)  12 us
    pallas_call x1, Pallas kernels, respond(): pl.pallas_call(response_kernel, in_specs=[pl.BlockSpec(memory_space=pltpu...  9.93 us
    pallas_call x1, Pallas kernels, dft(): pl.pallas_call(dft_kernel, in_specs=[pl.BlockSpec(memory_space=pltpu.SMEM...  7.33 us
    pallas_call x1, Pallas kernels, coefficients(): pl.pallas_call(coeff_kernel, in_specs=[pl.BlockSpec(memory_space=pltpu.SM...  6.72 us
    all_to_all x1, starting transfers between devices, on_device(): spectra = lax.all_to_all(local_spec, FREQ, 0, 0, tiled=True)  4.4 us
    ppermute x1, starting transfers between devices, on_device(): lax.ppermute(down, TILES, [(i, i + 1) for i in range(size - 1)])  3.81 us
  transfers between devices with their start and end apart: 3, of which 1 were waited for; matrix products, arithmetic and copies ran while one was open for 0% of the time, Pallas kernels for 5%

profile of v2, /device:TPU:0, one launch (start us, length us, event | category | flops | bytes accessed | tf_op | source)
XLA Modules:
  0.0 129.7 jit_solution(12037015201315220472)
XLA Ops:
  0.6 0.1 multiply_convert_fusion
  0.7 0.0 copy-start.3
  0.7 0.7 pad_maximum_fusion.tab_ref
  1.5 7.3 %shard_map.93 = bf16[8,2,2,16,768]{4,3,2,1,0:T(8,128)(2,1)} custom-call(s32[3,16]{1,0:T(4,128)} %bitcast.20, f32[256,256]{1,0:T(8,128)} %pad_maximum_fusion.tab_ref, bf16[16,128,768]{2,1,0:T(8,128)(2,1)} %plus_hbm.1, bf16[16,128,768]{2,1,0:T(8,128)(2,1)} %minus_hbm.1), custom_call_target="tpu_custom_call" | custom-call | flops 1610612736 | bytes 7340032 | tf_op jit(solution)/shard_map/pallas_call | solution.py:65
  8.8 4.4 %all-to-all-start = ((bf16[8,2,2,16,768]{4,3,2,1,0:T(8,128)(2,1)}), bf16[8,2,2,16,768]{4,3,2,1,0:T(8,128)(2,1)S(1)}, u32[]{:S(2)}, u32[]{:S(2)}) async-start(bf16[8,2,2,16,768]{4,3,2,1,0:T(8,128)(2,1)} %shard_map.93), calls=%async_computation | async-start | bytes 1572864 | tf_op jit(solution)/shard_map/all_to_all | solution.py:329
  13.2 0.0 copy-done.3
  13.2 0.6 copy.13
  13.8 12.6 %all-to-all-done.x_ref = bf16[8,2,2,16,768]{4,3,2,1,0:T(8,128)(2,1)S(1)} async-done(((bf16[8,2,2,16,768]{4,3,2,1,0:T(8,128)(2,1)}), bf16[8,2,2,16,768]{4,3,2,1,0:T(8,128)(2,1)S(1)}, u32[]{:S(2)}, u32[]{:S(2)}) %all-to-all-start) | async-done | bytes 786464 | tf_op jit(solution)/shard_map/all_to_all | solution.py:329
  26.4 0.0 copy-start
  26.4 0.9 copy-done
  27.2 3.4 %shard_map.94 = (bf16[3,3,32,512]{3,2,1,0:T(8,128)(2,1)}, bf16[32,512]{1,0:T(8,128)(2,1)}, bf16[32,512]{1,0:T(8,128)(2,1)}) custom-call(s32[1]{0:T(128)} %bitcast.place_ref, s32[3,48]{1,0:T(4,128)} %bitcast.18, bf16[8,2,2,16,768]{4,3,2,1,0:T(8,128)(2,1)} %copy-done, bf16[48,3,2,64,256]{4,3,2,1,0:T(8,128)(2,1)} %bitcast.12, ...), custom_call_target="tpu_custom_call" | custom-call | flops 150994944 | bytes 2097152 | tf_op jit(solution)/shard_map/pallas_call | solution.py:196
  30.6 3.8 %collective-permute-start = (bf16[32,512]{1,0:T(8,128)(2,1)}, bf16[32,512]{1,0:T(8,128)(2,1)S(1)}, u32[]{:S(2)}, u32[]{:S(2)}) collective-permute-start(bf16[32,512]{1,0:T(8,128)(2,1)} %get-tuple-element.17), channel_id=1, source_target_pairs={{0,1},{1,2},{2,3},{3,4},{4,5},{5,6},{6,7},{7,8},{8,9},{9,10},{10,1... | collective-permute-start | bytes 98312 | tf_op jit(solution)/shard_map/ppermute | solution.py:332
  34.5 1.3 collective-permute-start.1
  35.8 6.7 %shard_map.95 = bf16[16,3,3,32,512]{4,3,2,1,0:T(8,128)(2,1)} custom-call(s32[3,48]{1,0:T(4,128)} %bitcast.19, bf16[8,2,2,16,768]{4,3,2,1,0:T(8,128)(2,1)} %copy-done, bf16[48,3,2,64,256]{4,3,2,1,0:T(8,128)(2,1)} %bitcast.15), custom_call_target="tpu_custom_call" | custom-call | flops 2415919104 | bytes 10485760 | tf_op jit(solution)/shard_map/pallas_call | solution.py:124
  42.5 0.0 collective-permute-done.up_ref
  42.5 0.0 copy-start.1
  42.5 0.0 collective-permute-done.1.down_ref
  42.5 0.0 copy-start.2
  42.5 64.6 %all_to_all.15.c_hbm = bf16[16,3,3,32,512]{4,3,2,1,0:T(8,128)(2,1)} all-to-all(bf16[16,3,3,32,512]{4,3,2,1,0:T(8,128)(2,1)} %shard_map.95), channel_id=1, replica_groups=mesh['fx'=4,'fc'=2,'ty'=4,'tz'=4] {'ty','tz'}, dimensions={0} | all-to-all | bytes 9437184 | tf_op jit(solution)/shard_map/all_to_all | solution.py:337
  107.1 0.0 copy-done.1
  107.1 0.0 copy-done.2
  107.1 9.9 %shard_map.96 = (bf16[1,2,128,768]{3,2,1,0:T(8,128)(2,1)}, bf16[1,2,128,768]{3,2,1,0:T(8,128)(2,1)}, f32[16,2,2,8,128]{4,3,2,1,0:T(8,128)}) custom-call(s32[1]{0:T(128)} %bitcast.place_ref, bf16[16,3,3,32,512]{4,3,2,1,0:T(8,128)(2,1)} %all_to_all.15.c_hbm, bf16[3,48,2,64,256]{4,3,2,1,0:T(8,128)(2,1)} %bitcast.16, ...), custom_call_target="tpu_custom_call" | custom-call | flops 2415919104 | bytes 11534336 | tf_op jit(solution)/shard_map/pallas_call | solution.py:292
  117.0 12.0 %all_to_all.16 = f32[16,2,2,8,128]{4,3,2,1,0:T(8,128)S(1)} all-to-all(f32[16,2,2,8,128]{4,3,2,1,0:T(8,128)} %get-tuple-element.25), channel_id=1, replica_groups=mesh['fx'=4,'fc'=2,'ty'=4,'tz'=4] {'ty','tz'}, dimensions={0} | all-to-all | bytes 524288 | tf_op jit(solution)/shard_map/all_to_all | solution.py:339
  129.0 0.6 fusion.6
  (4 shorter events, 0.0 us)
Async XLA Ops:
  0.7 12.5 %copy-start.3 = (s32[1,48,3]{1,0,2:T(1,128)S(1)}, s32[1,48,3]{1,0,2:T(1,128)}, u32[]{:S(2)}) copy-start(s32[1,48,3]{1,0,2:T(1,128)} %param.9) | copy-start | bytes 1732
  8.8 17.6 %all-to-all-start = ((bf16[8,2,2,16,768]{4,3,2,1,0:T(8,128)(2,1)}), bf16[8,2,2,16,768]{4,3,2,1,0:T(8,128)(2,1)S(1)}, u32[]{:S(2)}, u32[]{:S(2)}) async-start(bf16[8,2,2,16,768]{4,3,2,1,0:T(8,128)(2,1)} %shard_map.93), calls=%async_computation | async-start | bytes 1572864 | tf_op jit(solution)/shard_map/all_to_all | solution.py:329
  26.4 0.9 copy-start
  30.6 11.8 %collective-permute-start = (bf16[32,512]{1,0:T(8,128)(2,1)}, bf16[32,512]{1,0:T(8,128)(2,1)S(1)}, u32[]{:S(2)}, u32[]{:S(2)}) collective-permute-start(bf16[32,512]{1,0:T(8,128)(2,1)} %get-tuple-element.17), channel_id=1, source_target_pairs={{0,1},{1,2},{2,3},{3,4},{4,5},{5,6},{6,7},{7,8},{8,9},{9,10},{10,1... | collective-permute-start | bytes 98312 | tf_op jit(solution)/shard_map/ppermute | solution.py:332
  34.5 8.1 %collective-permute-start.1 = (bf16[32,512]{1,0:T(8,128)(2,1)}, bf16[32,512]{1,0:T(8,128)(2,1)S(1)}, u32[]{:S(2)}, u32[]{:S(2)}) collective-permute-start(bf16[32,512]{1,0:T(8,128)(2,1)} %get-tuple-element.18), channel_id=1, source_target_pairs={{1,0},{2,1},{3,2},{4,3},{5,4},{6,5},{7,6},{8,7},{9,8},{10,9},{11,1... | collective-permute-start | bytes 98312 | tf_op jit(solution)/shard_map/ppermute | solution.py:333
  42.5 64.6 %copy-start.1 = (bf16[32,512]{1,0:T(8,128)(2,1)}, bf16[32,512]{1,0:T(8,128)(2,1)S(1)}, u32[]{:S(2)}) copy-start(bf16[32,512]{1,0:T(8,128)(2,1)S(1)} %collective-permute-done.up_ref) | copy-start | bytes 98308
  42.5 64.6 %copy-start.2 = (bf16[32,512]{1,0:T(8,128)(2,1)}, bf16[32,512]{1,0:T(8,128)(2,1)S(1)}, u32[]{:S(2)}) copy-start(bf16[32,512]{1,0:T(8,128)(2,1)S(1)} %collective-permute-done.1.down_ref) | copy-start | bytes 98308

commit v3 on v2

v3 whole, which is shorter than its diff:
```python
import functools
import math

import jax
import jax.numpy as jnp
from jax import lax
from jax.experimental import pallas as pl
from jax.experimental.pallas import tpu as pltpu
from jax.sharding import Mesh
from jax.sharding import PartitionSpec as P

R = 12288
GATE = 64
TILE = 256
HALF = 32
FREQ = ("fx", "fc")
TILES = ("ty", "tz")
BF = jnp.bfloat16
F32 = jnp.float32


def make_table(freq_count, sample_count):
    freq_ids = lax.broadcasted_iota(jnp.int32, (freq_count, sample_count), 0)
    sample_ids = lax.broadcasted_iota(jnp.int32, (freq_count, sample_count), 1)
    phase_ids = freq_ids * sample_ids % sample_count
    angles = phase_ids.astype(F32) * (2.0 * math.pi / sample_count)
    amplitude = 1.0 / math.sqrt(GATE)
    return jnp.stack([jnp.cos(angles) * amplitude, -jnp.sin(angles) * amplitude]).astype(BF)


def params(mib=56):
    return pltpu.CompilerParams(vmem_limit_bytes=mib * 2**20)


def dft_kernel(starts_ref, tab_ref, plus_ref, minus_ref, out_ref, rows_ref, t_ref):
    b = pl.program_id(0)

    @pl.when(b == 0)
    def _():
        rows = jnp.broadcast_to(tab_ref[...][:, None], (16, 16, 128)).reshape(256, 128)
        rows_ref[:, :128] = rows
        rows_ref[:, 128:] = rows

    lane = lax.broadcasted_iota(jnp.int32, (1, 256), 1)
    sample = lane & 127
    upper = lane >= 128
    row_source = lax.broadcasted_iota(jnp.int32, (256, 256), 0) & 15
    for p in range(8):
        start = jnp.where(upper, starts_ref[b, 2 * p + 1], starts_ref[b, 2 * p])
        inside = (sample >= start) & (sample < start + GATE)
        source = jnp.where(inside, jnp.where(upper, 2 * p + 1, 2 * p), -1)
        table = jnp.where(row_source == source, rows_ref[...], 0.0).astype(BF)
        t_ref[:, p * 256 : (p + 1) * 256] = table
    for q, ref in enumerate((plus_ref, minus_ref)):
        prod = jnp.dot(t_ref[...], ref[...].reshape(2048, 256), preferred_element_type=F32)
        prod = prod.reshape(8, 2, 16, 256)
        out_ref[:, 0, q] = prod[:, 0].astype(BF)
        out_ref[:, 1, q] = (prod[:, 1] if q == 0 else -prod[:, 1]).astype(BF)


def dft(plus_time, minus_time, gate_starts, table):
    sources, samples, receivers = plus_time.shape
    blocks = receivers // TILE
    data = pl.BlockSpec((sources, samples, TILE), lambda b: (0, 0, b))
    return pl.pallas_call(
        dft_kernel,
        grid=(blocks,),
        in_specs=[
            pl.BlockSpec(memory_space=pltpu.SMEM),
            pl.BlockSpec((16, 128), lambda b: (0, 0)),
            data,
            data,
        ],
        out_specs=pl.BlockSpec((8, 2, 2, 16, TILE), lambda b: (0, 0, 0, 0, b)),
        out_shape=jax.ShapeDtypeStruct((8, 2, 2, 16, receivers), BF),
        scratch_shapes=[pltpu.VMEM((256, 256), F32), pltpu.VMEM((256, 2048), BF)],
        compiler_params=params(),
        cost_estimate=pl.CostEstimate(
            flops=2 * 2 * 256 * 2048 * receivers, bytes_accessed=7 * 2**20, transcendentals=0
        ),
    )(gate_starts, table, plus_time, minus_time)


def fill_weights(w_ref, x_ref):
    for q in range(2):
        re = x_ref[:, 0, q].reshape(128, TILE).T
        im = x_ref[:, 1, q].reshape(128, TILE).T
        near, far = slice(q * 128, (q + 1) * 128), slice(256 + q * 128, 384 + q * 128)
        w_ref[0:256, near] = re
        w_ref[0:256, far] = im
        w_ref[256:512, near] = -im
        w_ref[256:512, far] = re


def coeff_kernel(
    place_ref, ranks_ref, x_ref, v_hbm, out_hbm, band_ref, v_ref, b_ref, o_ref, e_ref, w_ref, sems
):
    last_row = v_hbm.shape[0] - 1
    owners = out_hbm.shape[0]
    place = place_ref[0]

    def arrivals(j):
        low = v_hbm.at[:, j, :, pl.ds(0, HALF), :]
        copies = [pltpu.make_async_copy(low, v_ref.at[j], sems.at[j, 0])]
        for n in range(3):
            i = jnp.clip(place * 3 + j + n - 1, 0, last_row)
            src = v_hbm.at[i, j, :, pl.ds(HALF, HALF), :]
            copies.append(pltpu.make_async_copy(src, b_ref.at[j, n], sems.at[j, 1 + n]))
        return copies

    def sends(j):
        return [
            pltpu.make_async_copy(o_ref.at[j, i], out_hbm.at[:, 3 * i + j], sems.at[j, 4 + i])
            for i in range(3)
        ]

    def edge(side):
        to = jnp.clip(place + 2 * side - 1, 0, owners - 1)
        return pltpu.make_async_copy(e_ref.at[side], out_hbm.at[to, 9], sems.at[side, 7])

    for copy in arrivals(0):
        copy.start()
    rank_ids = lax.broadcasted_iota(jnp.int32, (HALF, 512), 0)
    band_ref[0, 0] = jnp.zeros((HALF, 512), BF)
    band_ref[2, 2] = jnp.zeros((HALF, 512), BF)
    for j in range(3):
        if j < 2:
            for copy in arrivals(j + 1):
                copy.start()
        fill_weights(w_ref, x_ref.at[:, :, :, :, pl.ds(j * TILE, TILE)])
        for copy in arrivals(j):
            copy.wait()
        v = jnp.concatenate([b_ref[j, :, c].reshape(3 * HALF, TILE) for c in range(2)], axis=1)
        prod = jnp.dot(v, w_ref[...], preferred_element_type=F32)
        for n in range(3):
            i = place * 3 + j + n - 1
            rank = ranks_ref[j, jnp.clip(i, 0, last_row)]
            kept = jnp.where(rank_ids + HALF < rank, prod[n * HALF : (n + 1) * HALF], 0.0).astype(BF)
            il = j + n - 1
            if il < 0:
                e_ref[0] = kept
            elif il > 2:
                e_ref[1] = kept
            else:
                band_ref[il, 2 - n] = kept
        for h in range(4):
            rows = slice(h * 12, (h + 1) * 12)
            v = jnp.concatenate([v_ref[j, rows, c].reshape(12 * HALF, TILE) for c in range(2)], axis=1)
            prod = jnp.dot(v, w_ref[...], preferred_element_type=F32)
            for n in range(12):
                i = h * 12 + n
                kept = jnp.where(rank_ids < ranks_ref[j, i], prod[n * HALF : (n + 1) * HALF], 0.0)
                o_ref[j, i % 3, i // 3] = kept.astype(BF)
        for copy in sends(j):
            copy.start()

    @pl.when(place > 0)
    def _():
        edge(0).start()

    @pl.when(place < owners - 1)
    def _():
        edge(1).start()

    for j in range(3):
        for copy in sends(j):
            copy.wait()

    @pl.when(place > 0)
    def _():
        edge(0).wait()

    @pl.when(place < owners - 1)
    def _():
        edge(1).wait()


def coefficients(spectra, v_factors, ranks, place):
    rows, cols = v_factors.shape[:2]
    whole = pl.BlockSpec(memory_space=pltpu.VMEM)
    scalars = pl.BlockSpec(memory_space=pltpu.SMEM)
    return pl.pallas_call(
        coeff_kernel,
        in_specs=[scalars, scalars, whole, pl.BlockSpec(memory_space=pl.ANY)],
        out_specs=[pl.BlockSpec(memory_space=pl.ANY), whole],
        out_shape=[
            jax.ShapeDtypeStruct((rows // 3, 10, HALF, 512), BF),
            jax.ShapeDtypeStruct((3, 3, HALF, 512), BF),
        ],
        scratch_shapes=[
            pltpu.VMEM((cols, rows, 2, HALF, TILE), BF),
            pltpu.VMEM((cols, 3, 2, HALF, TILE), BF),
            pltpu.VMEM((cols, 3, rows // 3, HALF, 512), BF),
            pltpu.VMEM((2, HALF, 512), BF),
            pltpu.VMEM((512, 512), BF),
            pltpu.SemaphoreType.DMA((3, 8)),
        ],
        compiler_params=params(52),
        cost_estimate=pl.CostEstimate(
            flops=2 * rows * cols * HALF * 512 * 512, bytes_accessed=10 * 2**20, transcendentals=0
        ),
    )(place, ranks, spectra, v_factors)


def response_kernel(
    place_ref, c_hbm, u_hbm, band_ref, minus_hbm, plus_hbm, gram_ref,
    c_ref, u_ref, cb_ref, ub_ref, z_ref, acc, sems,
):
    all_cols = u_hbm.shape[1]
    owners = c_hbm.shape[0]
    place = place_ref[0]
    parts = ((0, owners // 2), (owners // 2, owners - owners // 2))

    def arrivals(i, g):
        first, count = parts[g]
        cols = pl.ds(3 * first, 3 * count)
        pairs = [
            (c_hbm.at[pl.ds(first, count), pl.ds(3 * i, 3)], c_ref.at[i, pl.ds(first, count)]),
            (u_hbm.at[i, cols, :, pl.ds(0, HALF), :], u_ref.at[i, cols]),
        ]
        if g == 1:
            for n in range(3):
                col = jnp.clip(place * 3 + i + n - 1, 0, all_cols - 1)
                pairs.append((u_hbm.at[i, col, :, pl.ds(HALF, HALF), :], ub_ref.at[i, n]))
            if i == 0:
                below = jnp.maximum(place - 1, 0)
                pairs.append((c_hbm.at[below, 9], cb_ref.at[i, 0]))
            if i == 2:
                above = jnp.minimum(place + 1, owners - 1)
                pairs.append((c_hbm.at[above, 9], cb_ref.at[i, 2]))
        at = [2 * g + k for k in range(len(pairs))]
        return [pltpu.make_async_copy(s, d, sems.at[i, k]) for k, (s, d) in zip(at, pairs)]

    def sends(i):
        lanes = pl.ds(i * TILE, TILE)
        return [
            pltpu.make_async_copy(z_ref.at[i, n], ref.at[0, :, :, lanes], sems.at[i, 8 + n])
            for n, ref in enumerate((minus_hbm, plus_hbm))
        ]

    def product(left, right):
        depth = left.shape[0] * HALF
        right = jnp.concatenate([right[:, c].reshape(depth, TILE) for c in range(2)], axis=1)
        left = left.reshape(depth, 512)
        return lax.dot_general(left, right, (((0,), (0,)), ((), ())), preferred_element_type=F32)

    for g in range(2):
        for copy in arrivals(0, g):
            copy.start()
    for i in range(3):
        for n in range(3):
            if (i, n) not in ((0, 0), (2, 2)):
                cb_ref[i, n] = band_ref[i, n]
        cb_ref[i, 3] = jnp.zeros((HALF, 512), BF)
        ub_ref[i, 3] = jnp.zeros((2, HALF, TILE), BF)
    for i in range(3):
        if i < 2:
            for g in range(2):
                for copy in arrivals(i + 1, g):
                    copy.start()
        for copy in arrivals(i, 0):
            copy.wait()
        if i == 0:
            mid = owners // 2
            acc[...] = product(c_ref[0, :mid].reshape(3 * mid, HALF, 512), u_ref[0, : 3 * mid])
        for copy in arrivals(i, 1):
            copy.wait()
        if i == 0:
            cb_ref[0, 0] = jnp.where(place > 0, cb_ref[0, 0], jnp.zeros((), BF))
        if i == 2:
            cb_ref[2, 2] = jnp.where(place < owners - 1, cb_ref[2, 2], jnp.zeros((), BF))
        first = owners // 2 if i == 0 else 0
        prod = product(
            c_ref[i, first:].reshape(3 * (owners - first), HALF, 512), u_ref[i, 3 * first :]
        )
        if i == 0:
            prod += acc[...]
        prod += product(cb_ref[i], ub_ref[i])
        re = (prod[:256, :256] - prod[256:, 256:]).astype(BF)
        im = prod[256:, :256] + prod[:256, 256:]
        im = jnp.concatenate([im[:128], -im[128:]], axis=0).astype(BF)
        z_ref[i, 0, 0] = re[:128]
        z_ref[i, 0, 1] = im[:128]
        z_ref[i, 1, 0] = re[128:]
        z_ref[i, 1, 1] = im[128:]
        for copy in sends(i):
            copy.start()
    rows = [jnp.concatenate([z_ref[i, m, c] for i in range(3)], axis=1) for c in range(2) for m in range(2)]
    gram = lax.dot_general(
        jnp.concatenate(rows, axis=0),
        jnp.concatenate([rows[1], rows[3]], axis=0),
        (((1,), (1,)), ((), ())),
        preferred_element_type=F32,
    )
    parts = (gram[:256, :128] + gram[256:, 128:], gram[256:, :128] - gram[:256, 128:])
    for m, scale in enumerate((1.0 / math.sqrt(R), 1.0 / R)):
        for c, part in enumerate(parts):
            gram_ref[:, m, c] = (part[m * 128 : (m + 1) * 128] * scale).reshape(16, 8, 128)
    for i in range(3):
        for copy in sends(i):
            copy.wait()


def respond(coeffs, u_factors, band, place):
    rows, all_cols = u_factors.shape[:2]
    whole = pl.BlockSpec(memory_space=pltpu.VMEM)
    anywhere = pl.BlockSpec(memory_space=pl.ANY)
    return pl.pallas_call(
        response_kernel,
        in_specs=[pl.BlockSpec(memory_space=pltpu.SMEM), anywhere, anywhere, whole],
        out_specs=[anywhere, anywhere, whole],
        scratch_shapes=[
            pltpu.VMEM((rows, all_cols // 3, 3, HALF, 512), BF),
            pltpu.VMEM((rows, all_cols, 2, HALF, TILE), BF),
            pltpu.VMEM((rows, 4, HALF, 512), BF),
            pltpu.VMEM((rows, 4, 2, HALF, TILE), BF),
            pltpu.VMEM((rows, 2, 2, 128, TILE), BF),
            pltpu.VMEM((512, 512), F32),
            pltpu.SemaphoreType.DMA((3, 10)),
        ],
        out_shape=[
            jax.ShapeDtypeStruct((1, 2, 128, rows * TILE), BF),
            jax.ShapeDtypeStruct((1, 2, 128, rows * TILE), BF),
            jax.ShapeDtypeStruct((16, 2, 2, 8, 128), F32),
        ],
        compiler_params=params(),
        cost_estimate=pl.CostEstimate(
            flops=2 * 144 * HALF * 512 * 512, bytes_accessed=11 * 2**20, transcendentals=0
        ),
    )(place, coeffs, u_factors, band)


def on_device(plus_time, minus_time, gate_starts, tile_ranks, u_factors, v_factors):
    u_factors, v_factors, ranks = u_factors[0], v_factors[0], tile_ranks[0].T
    place = lax.axis_index(TILES).astype(jnp.int32).reshape(1)
    rows = make_table(8, 128).astype(F32).transpose(1, 0, 2)
    local_spec = dft(plus_time, minus_time, gate_starts.T, rows.reshape(16, 128))
    spectra = lax.all_to_all(local_spec, FREQ, 0, 0, tiled=True)
    coeffs, band = coefficients(spectra, v_factors, ranks, place)
    arrived = lax.all_to_all(coeffs, TILES, 0, 0, tiled=True)
    minus_new, plus_new, gram = respond(arrived, u_factors, band, place)
    sums = lax.all_to_all(gram, TILES, 0, 0, tiled=True).sum(axis=0)
    return (minus_new, plus_new, sums[None, 0], sums[None, 1])


def solution(mesh):
    torus = Mesh(mesh.devices.reshape(4, 2, 4, 4), (*FREQ, *TILES))
    in_specs = (
        P(FREQ, None, TILES),
        P(FREQ, None, TILES),
        P(FREQ, TILES),
        P(FREQ, None, TILES),
        P(FREQ, TILES, None, None, None, None),
        P(FREQ, None, TILES, None, None, None),
    )
    out_specs = (
        P(FREQ, None, None, TILES),
        P(FREQ, None, None, TILES),
        P(FREQ, None, TILES, None),
        P(FREQ, None, TILES, None),
    )
    return jax.shard_map(
        on_device, mesh=torus, in_specs=in_specs, out_specs=out_specs, check_vma=False
    )
```

time: 130 us -> 125 us (0.962)
  blocking collectives: 76.5 us -> 82 us
  starting transfers between devices: 9.5 us -> 4.38 us
  Pallas kernels: 27.4 us -> 23.1 us
    all_to_all x1, blocking collectives: 64.6 us -> 70 us  [on_device(): arrived = lax.all_to_all(coeffs, TILES, 0, 0, tiled=True)]
    ppermute x2 -> x0, starting transfers between devices: 5.1 us -> none  [the longest x1 3.81 us: on_device(): lax.ppermute(down, TILES, [(i, i + 1) for i in range(size - 1)])]
    pallas_call x3 -> x2, Pallas kernels: 17.5 us -> 12.9 us  [the longest x1 7.5 us: coefficients(): pl.pallas_call(coeff_kernel, in_specs=[scalars, scalars, whole, pl.BlockS...]
    unnamed x9 -> x5, local copies, waits for them, and re-layouts: 1.48 us -> 0.01 us
  transfers between devices with their start and end apart: 3 -> 1, of which waited for: 1 -> 1; matrix products, arithmetic and copies ran while one was open for 0% -> 0% of each run, Pallas kernels for 5% -> 0%
where the time goes in v3:
time: 125 us
  blocking collectives  82 us (66%)
  Pallas kernels  23.1 us (18%)
  waiting for transfers between devices  13.1 us (10%)
  starting transfers between devices  4.38 us (4%)
    all_to_all x1, blocking collectives, on_device(): arrived = lax.all_to_all(coeffs, TILES, 0, 0, tiled=True)  70 us
    all_to_all x1, waiting for transfers between devices, on_device(): spectra = lax.all_to_all(local_spec, FREQ, 0, 0, tiled=True)  13.1 us
    all_to_all x1, blocking collectives, on_device(): sums = lax.all_to_all(gram, TILES, 0, 0, tiled=True).sum(axis=0)  12 us
    pallas_call x1, Pallas kernels, respond(): pl.pallas_call(response_kernel, in_specs=[pl.BlockSpec(memory_space=pltpu...  10.1 us
    pallas_call x1, Pallas kernels, coefficients(): pl.pallas_call(coeff_kernel, in_specs=[scalars, scalars, whole, pl.BlockS...  7.5 us
    pallas_call x1, Pallas kernels, dft(): pl.pallas_call(dft_kernel, grid=(blocks,), in_specs=[pl.BlockSpec(memory_...  5.43 us
    all_to_all x1, starting transfers between devices, on_device(): spectra = lax.all_to_all(local_spec, FREQ, 0, 0, tiled=True)  4.38 us
  transfers between devices with their start and end apart: 1, of which 1 were waited for; matrix products, arithmetic and copies ran while one was open for 0% of the time, Pallas kernels for 0%

profile of v3, /device:TPU:0, one launch (start us, length us, event | category | flops | bytes accessed | tf_op | source)
XLA Modules:
  0.0 124.6 jit_solution(17383578034083916904)
XLA Ops:
  0.6 0.0 copy-start.1
  0.6 0.1 multiply_convert_fusion
  0.7 0.6 copy.10
  1.3 5.4 %shard_map.93 = bf16[8,2,2,16,768]{4,3,2,1,0:T(8,128)(2,1)} custom-call(s32[3,16]{1,0:T(4,128)} %bitcast.16, f32[16,128]{1,0:T(8,128)} %bitcast.15, bf16[16,128,768]{2,1,0:T(8,128)(2,1)} %plus_ref.1, bf16[16,128,768]{2,1,0:T(8,128)(2,1)} %minus_ref.1), custom_call_target="tpu_custom_call" | custom-call | flops 1610612736 | bytes 7340032 | tf_op jit(solution)/shard_map/pallas_call | solution.py:65
  6.8 4.4 %all-to-all-start = ((bf16[8,2,2,16,768]{4,3,2,1,0:T(8,128)(2,1)}), bf16[8,2,2,16,768]{4,3,2,1,0:T(8,128)(2,1)S(1)}, u32[]{:S(2)}, u32[]{:S(2)}) async-start(bf16[8,2,2,16,768]{4,3,2,1,0:T(8,128)(2,1)} %shard_map.93), calls=%async_computation | async-start | bytes 1572864 | tf_op jit(solution)/shard_map/all_to_all | solution.py:338
  11.1 0.0 copy-done.1
  11.2 13.1 %all-to-all-done.x_ref = bf16[8,2,2,16,768]{4,3,2,1,0:T(8,128)(2,1)S(1)} async-done(((bf16[8,2,2,16,768]{4,3,2,1,0:T(8,128)(2,1)}), bf16[8,2,2,16,768]{4,3,2,1,0:T(8,128)(2,1)S(1)}, u32[]{:S(2)}, u32[]{:S(2)}) %all-to-all-start) | async-done | bytes 786464 | tf_op jit(solution)/shard_map/all_to_all | solution.py:338
  24.3 7.5 %shard_map.94 = (bf16[16,10,32,512]{3,2,1,0:T(8,128)(2,1)}, bf16[3,3,32,512]{3,2,1,0:T(8,128)(2,1)S(1)}) custom-call(s32[1]{0:T(128)} %bitcast.place_ref, s32[3,48]{1,0:T(4,128)S(1)} %bitcast.12, bf16[8,2,2,16,768]{4,3,2,1,0:T(8,128)(2,1)S(1)} %all-to-all-done.x_ref, bf16[48,3,2,64,256]{4,3,2,1,0:T(8,128)(2,1)} %bitcast.13), custom_call_target="tpu_custom_call" | custom-call | flops 2415919104 | bytes 10485760 | tf_op jit(solution)/shard_map/pallas_call | solution.py:182
  31.8 0.0 copy-start
  31.8 70.0 %all_to_all.15.c_hbm = bf16[16,10,32,512]{3,2,1,0:T(8,128)(2,1)} all-to-all(bf16[16,10,32,512]{3,2,1,0:T(8,128)(2,1)} %get-tuple-element.9), channel_id=1, replica_groups=mesh['fx'=4,'fc'=2,'ty'=4,'tz'=4] {'ty','tz'}, dimensions={0} | all-to-all | bytes 10485760 | tf_op jit(solution)/shard_map/all_to_all | solution.py:340
  101.8 0.0 copy-done
  101.8 10.1 %shard_map.95 = (bf16[1,2,128,768]{3,2,1,0:T(8,128)(2,1)}, bf16[1,2,128,768]{3,2,1,0:T(8,128)(2,1)}, f32[16,2,2,8,128]{4,3,2,1,0:T(8,128)}) custom-call(s32[1]{0:T(128)} %bitcast.place_ref, bf16[16,10,32,512]{3,2,1,0:T(8,128)(2,1)} %all_to_all.15.c_hbm, bf16[3,48,2,64,256]{4,3,2,1,0:T(8,128)(2,1)} %bitcast.14, bf16[3,3,32,512]{3,2,1,0:T(8,128)(2,1)} %copy-done), custom_call_target="tpu_custom_call" | custom-call | flops 2415919104 | bytes 11534336 | tf_op jit(solution)/shard_map/pallas_call | solution.py:308
  112.0 12.0 %all_to_all.16 = f32[16,2,2,8,128]{4,3,2,1,0:T(8,128)S(1)} all-to-all(f32[16,2,2,8,128]{4,3,2,1,0:T(8,128)} %get-tuple-element.13), channel_id=1, replica_groups=mesh['fx'=4,'fc'=2,'ty'=4,'tz'=4] {'ty','tz'}, dimensions={0} | all-to-all | bytes 524288 | tf_op jit(solution)/shard_map/all_to_all | solution.py:342
  124.0 0.6 fusion.6
  (3 shorter events, 0.0 us)
Async XLA Ops:
  0.6 10.5 %copy-start.1 = (s32[1,48,3]{1,0,2:T(1,128)S(1)}, s32[1,48,3]{1,0,2:T(1,128)}, u32[]{:S(2)}) copy-start(s32[1,48,3]{1,0,2:T(1,128)} %param.9) | copy-start | bytes 1732
  6.8 17.5 %all-to-all-start = ((bf16[8,2,2,16,768]{4,3,2,1,0:T(8,128)(2,1)}), bf16[8,2,2,16,768]{4,3,2,1,0:T(8,128)(2,1)S(1)}, u32[]{:S(2)}, u32[]{:S(2)}) async-start(bf16[8,2,2,16,768]{4,3,2,1,0:T(8,128)(2,1)} %shard_map.93), calls=%async_computation | async-start | bytes 1572864 | tf_op jit(solution)/shard_map/all_to_all | solution.py:338
  31.8 70.0 %copy-start = (bf16[3,3,32,512]{3,2,1,0:T(8,128)(2,1)}, bf16[3,3,32,512]{3,2,1,0:T(8,128)(2,1)S(1)}, u32[]{:S(2)}) copy-start(bf16[3,3,32,512]{3,2,1,0:T(8,128)(2,1)S(1)} %get-tuple-element.10.band_ref) | copy-start | bytes 884740

commit v4 on v3

--- a/solution.py
+++ b/solution.py
@@ -79,6 +79,24 @@
             flops=2 * 2 * 256 * 2048 * receivers, bytes_accessed=7 * 2**20, transcendentals=0
         ),
     )(gate_starts, table, plus_time, minus_time)
+
+
+def hold_kernel(u_hbm, u_ref, sem):
+    copy = pltpu.make_async_copy(u_hbm.at[:, :, :, pl.ds(0, HALF), :], u_ref, sem)
+    copy.start()
+    copy.wait()
+
+
+def held(u_factors):
+    return pl.pallas_call(
+        hold_kernel,
+        in_specs=[pl.BlockSpec(memory_space=pl.ANY)],
+        out_specs=pl.BlockSpec(memory_space=pltpu.VMEM),
+        out_shape=pltpu.VMEM((*u_factors.shape[:3], HALF, TILE), BF),
+        scratch_shapes=[pltpu.SemaphoreType.DMA],
+        compiler_params=params(52),
+        cost_estimate=pl.CostEstimate(flops=0, bytes_accessed=5 * 2**20, transcendentals=0),
+    )(u_factors)
 
 
 def fill_weights(w_ref, x_ref):
@@ -203,8 +221,8 @@
 
 
 def response_kernel(
-    place_ref, c_hbm, u_hbm, band_ref, minus_hbm, plus_hbm, gram_ref,
-    c_ref, u_ref, cb_ref, ub_ref, z_ref, acc, sems,
+    place_ref, c_hbm, u_ref, u_hbm, band_ref, minus_hbm, plus_hbm, gram_ref,
+    c_ref, cb_ref, ub_ref, z_ref, acc, sems,
 ):
     all_cols = u_hbm.shape[1]
     owners = c_hbm.shape[0]
@@ -213,10 +231,8 @@
 
     def arrivals(i, g):
         first, count = parts[g]
-        cols = pl.ds(3 * first, 3 * count)
         pairs = [
             (c_hbm.at[pl.ds(first, count), pl.ds(3 * i, 3)], c_ref.at[i, pl.ds(first, count)]),
-            (u_hbm.at[i, cols, :, pl.ds(0, HALF), :], u_ref.at[i, cols]),
         ]
         if g == 1:
             for n in range(3):
@@ -301,17 +317,16 @@
             copy.wait()
 
 
-def respond(coeffs, u_factors, band, place):
+def respond(coeffs, u_held, u_factors, band, place):
     rows, all_cols = u_factors.shape[:2]
     whole = pl.BlockSpec(memory_space=pltpu.VMEM)
     anywhere = pl.BlockSpec(memory_space=pl.ANY)
     return pl.pallas_call(
         response_kernel,
-        in_specs=[pl.BlockSpec(memory_space=pltpu.SMEM), anywhere, anywhere, whole],
+        in_specs=[pl.BlockSpec(memory_space=pltpu.SMEM), anywhere, whole, anywhere, whole],
         out_specs=[anywhere, anywhere, whole],
         scratch_shapes=[
             pltpu.VMEM((rows, all_cols // 3, 3, HALF, 512), BF),
-            pltpu.VMEM((rows, all_cols, 2, HALF, TILE), BF),
             pltpu.VMEM((rows, 4, HALF, 512), BF),
             pltpu.VMEM((rows, 4, 2, HALF, TILE), BF),
             pltpu.VMEM((rows, 2, 2, 128, TILE), BF),
@@ -323,11 +338,11 @@
             jax.ShapeDtypeStruct((1, 2, 128, rows * TILE), BF),
             jax.ShapeDtypeStruct((16, 2, 2, 8, 128), F32),
         ],
-        compiler_params=params(),
+        compiler_params=params(40),
         cost_estimate=pl.CostEstimate(
             flops=2 * 144 * HALF * 512 * 512, bytes_accessed=11 * 2**20, transcendentals=0
         ),
-    )(place, coeffs, u_factors, band)
+    )(place, coeffs, u_held, u_factors, band)
 
 
 def on_device(plus_time, minus_time, gate_starts, tile_ranks, u_factors, v_factors):
@@ -336,9 +351,10 @@
     rows = make_table(8, 128).astype(F32).transpose(1, 0, 2)
     local_spec = dft(plus_time, minus_time, gate_starts.T, rows.reshape(16, 128))
     spectra = lax.all_to_all(local_spec, FREQ, 0, 0, tiled=True)
+    spectra, u_held = lax.optimization_barrier((spectra, held(u_factors)))
     coeffs, band = coefficients(spectra, v_factors, ranks, place)
     arrived = lax.all_to_all(coeffs, TILES, 0, 0, tiled=True)
-    minus_new, plus_new, gram = respond(arrived, u_factors, band, place)
+    minus_new, plus_new, gram = respond(arrived, u_held, u_factors, band, place)
     sums = lax.all_to_all(gram, TILES, 0, 0, tiled=True).sum(axis=0)
     return (minus_new, plus_new, sums[None, 0], sums[None, 1])
 

time: 125 us -> 122 us (0.976)
  waiting for transfers between devices: 13.1 us -> 8.62 us
  local copies, waits for them, and re-layouts: 1.22 us -> 3.38 us
    all_to_all x1, waiting for transfers between devices: 13.1 us -> 8.62 us  [on_device(): spectra = lax.all_to_all(local_spec, FREQ, 0, 0, tiled=True)]
    pallas_call x1, Pallas kernels: 10.1 us -> 6.97 us  [respond(): pl.pallas_call(response_kernel, in_specs=[pl.BlockSpec(memory_space=pltpu...]
    pallas_call x0 -> x1, Pallas kernels: none -> 2.35 us  [held(): pl.pallas_call(hold_kernel, in_specs=[pl.BlockSpec(memory_space=pl.ANY)],...]
    unnamed x5 -> x9, local copies, waits for them, and re-layouts: 0.01 us -> 2.17 us
  transfers between devices with their start and end apart: 1 -> 1, of which waited for: 1 -> 1; matrix products, arithmetic and copies ran while one was open for 0% -> 0% of each run, Pallas kernels for 0% -> 2%
where the time goes in v4:
time: 122 us; the launch traced here: 121 us
  blocking collectives  81.9 us (67%)
  Pallas kernels  22.2 us (18%)
  waiting for transfers between devices  8.62 us (7%)
  starting transfers between devices  4.38 us (4%)
  local copies, waits for them, and re-layouts  3.38 us (3%)
    all_to_all x1, blocking collectives, on_device(): arrived = lax.all_to_all(coeffs, TILES, 0, 0, tiled=True)  70.2 us
    all_to_all x1, blocking collectives, on_device(): sums = lax.all_to_all(gram, TILES, 0, 0, tiled=True).sum(axis=0)  11.8 us
    all_to_all x1, waiting for transfers between devices, on_device(): spectra = lax.all_to_all(local_spec, FREQ, 0, 0, tiled=True)  8.62 us
    pallas_call x1, Pallas kernels, coefficients(): pl.pallas_call(coeff_kernel, in_specs=[scalars, scalars, whole, pl.BlockS...  7.5 us
    pallas_call x1, Pallas kernels, respond(): pl.pallas_call(response_kernel, in_specs=[pl.BlockSpec(memory_space=pltpu...  6.97 us
    pallas_call x1, Pallas kernels, dft(): pl.pallas_call(dft_kernel, grid=(blocks,), in_specs=[pl.BlockSpec(memory_...  5.43 us
    all_to_all x1, starting transfers between devices, on_device(): spectra = lax.all_to_all(local_spec, FREQ, 0, 0, tiled=True)  4.38 us
  transfers between devices with their start and end apart: 1, of which 1 were waited for; matrix products, arithmetic and copies ran while one was open for 0% of the time, Pallas kernels for 2%

profile of v4, /device:TPU:0, one launch (start us, length us, event | category | flops | bytes accessed | tf_op | source)
XLA Modules:
  0.0 121.4 jit_solution(5093852453593275649)
XLA Ops:
  0.6 0.0 copy-start.1
  0.6 0.1 multiply_convert_fusion
  0.7 0.6 copy.10
  1.3 5.4 %shard_map.93 = bf16[8,2,2,16,768]{4,3,2,1,0:T(8,128)(2,1)} custom-call(s32[3,16]{1,0:T(4,128)} %bitcast.19, f32[16,128]{1,0:T(8,128)} %bitcast.18, bf16[16,128,768]{2,1,0:T(8,128)(2,1)} %plus_ref.1, bf16[16,128,768]{2,1,0:T(8,128)(2,1)} %minus_ref.1), custom_call_target="tpu_custom_call" | custom-call | flops 1610612736 | bytes 7340032 | tf_op jit(solution)/shard_map/pallas_call | solution.py:65
  6.7 4.4 %all-to-all-start = ((bf16[8,2,2,16,768]{4,3,2,1,0:T(8,128)(2,1)}), bf16[8,2,2,16,768]{4,3,2,1,0:T(8,128)(2,1)S(1)}, u32[]{:S(2)}, u32[]{:S(2)}) async-start(bf16[8,2,2,16,768]{4,3,2,1,0:T(8,128)(2,1)} %shard_map.93), calls=%async_computation | async-start | bytes 1572864 | tf_op jit(solution)/shard_map/all_to_all | solution.py:353
  11.1 0.0 copy-done.1
  11.1 2.3 %shard_map.94.u_ref = bf16[3,48,2,32,256]{4,3,2,1,0:T(8,128)(2,1)S(1)} custom-call(bf16[3,48,2,64,256]{4,3,2,1,0:T(8,128)(2,1)} %bitcast.15), custom_call_target="tpu_custom_call" | custom-call | bytes 5242880 | tf_op jit(solution)/shard_map/pallas_call | solution.py:91
  13.5 0.0 copy-start
  13.5 2.2 %copy-done = bf16[3,48,2,32,256]{4,3,2,1,0:T(8,128)(2,1)} copy-done((bf16[3,48,2,32,256]{4,3,2,1,0:T(8,128)(2,1)}, bf16[3,48,2,32,256]{4,3,2,1,0:T(8,128)(2,1)S(1)}, u32[]{:S(2)}) %copy-start) | copy-done | bytes 4718616
  15.7 8.6 %all-to-all-done.x_ref = bf16[8,2,2,16,768]{4,3,2,1,0:T(8,128)(2,1)S(1)} async-done(((bf16[8,2,2,16,768]{4,3,2,1,0:T(8,128)(2,1)}), bf16[8,2,2,16,768]{4,3,2,1,0:T(8,128)(2,1)S(1)}, u32[]{:S(2)}, u32[]{:S(2)}) %all-to-all-start) | async-done | bytes 786464 | tf_op jit(solution)/shard_map/all_to_all | solution.py:353
  24.3 0.0 slice-start
  24.3 7.5 %shard_map.95 = (bf16[16,10,32,512]{3,2,1,0:T(8,128)(2,1)}, bf16[3,3,32,512]{3,2,1,0:T(8,128)(2,1)S(1)}) custom-call(s32[1]{0:T(128)} %bitcast.place_ref, s32[3,48]{1,0:T(4,128)S(1)} %bitcast.14, bf16[8,2,2,16,768]{4,3,2,1,0:T(8,128)(2,1)S(1)} %all-to-all-done.x_ref, bf16[48,3,2,64,256]{4,3,2,1,0:T(8,128)(2,1)} %bitcast.17), custom_call_target="tpu_custom_call" | custom-call | flops 2415919104 | bytes 10485760 | tf_op jit(solution)/shard_map/pallas_call | solution.py:200
  31.8 0.0 slice-start.1
  31.8 70.2 %all_to_all.15.c_hbm = bf16[16,10,32,512]{3,2,1,0:T(8,128)(2,1)S(1)} all-to-all(bf16[16,10,32,512]{3,2,1,0:T(8,128)(2,1)} %get-tuple-element.12), channel_id=1, replica_groups=mesh['fx'=4,'fc'=2,'ty'=4,'tz'=4] {'ty','tz'}, dimensions={0} | all-to-all | bytes 10485760 | tf_op jit(solution)/shard_map/all_to_all | solution.py:356
  102.0 0.0 slice-done
  102.0 0.0 slice-done.1
  102.0 7.0 %shard_map.96 = (bf16[1,2,128,768]{3,2,1,0:T(8,128)(2,1)}, bf16[1,2,128,768]{3,2,1,0:T(8,128)(2,1)}, f32[16,2,2,8,128]{4,3,2,1,0:T(8,128)S(1)}) custom-call(s32[1]{0:T(128)} %bitcast.place_ref, bf16[16,10,32,512]{3,2,1,0:T(8,128)(2,1)S(1)} %all_to_all.15.c_hbm, bf16[3,48,2,32,256]{4,3,2,1,0:T(8,128)(2,1)S(1)} %bitcast.13, ...), custom_call_target="tpu_custom_call" | custom-call | flops 2415919104 | bytes 11534336 | tf_op jit(solution)/shard_map/pallas_call | solution.py:324
  109.0 11.8 %all_to_all.16 = f32[16,2,2,8,128]{4,3,2,1,0:T(8,128)S(1)} all-to-all(f32[16,2,2,8,128]{4,3,2,1,0:T(8,128)S(1)} %get-tuple-element.17), channel_id=1, replica_groups=mesh['fx'=4,'fc'=2,'ty'=4,'tz'=4] {'ty','tz'}, dimensions={0} | all-to-all | bytes 524288 | tf_op jit(solution)/shard_map/all_to_all | solution.py:358
  120.8 0.6 fusion.6
  (4 shorter events, 0.0 us)
Async XLA Ops:
  0.6 10.5 %copy-start.1 = (s32[1,48,3]{1,0,2:T(1,128)S(1)}, s32[1,48,3]{1,0,2:T(1,128)}, u32[]{:S(2)}) copy-start(s32[1,48,3]{1,0,2:T(1,128)} %param.9) | copy-start | bytes 1732
  6.7 17.5 %all-to-all-start = ((bf16[8,2,2,16,768]{4,3,2,1,0:T(8,128)(2,1)}), bf16[8,2,2,16,768]{4,3,2,1,0:T(8,128)(2,1)S(1)}, u32[]{:S(2)}, u32[]{:S(2)}) async-start(bf16[8,2,2,16,768]{4,3,2,1,0:T(8,128)(2,1)} %shard_map.93), calls=%async_computation | async-start | bytes 1572864 | tf_op jit(solution)/shard_map/all_to_all | solution.py:353
  13.5 2.2 %copy-start = (bf16[3,48,2,32,256]{4,3,2,1,0:T(8,128)(2,1)}, bf16[3,48,2,32,256]{4,3,2,1,0:T(8,128)(2,1)S(1)}, u32[]{:S(2)}) copy-start(bf16[3,48,2,32,256]{4,3,2,1,0:T(8,128)(2,1)S(1)} %shard_map.94.u_ref) | copy-start | bytes 14155780
  24.3 77.7 %slice-start = ((s8[4718592]{0:T(1024)(128)(4,1)}), s8[524288]{0:T(1024)(128)(4,1)S(1)}, s32[]{:S(2)}) async-start(s8[4718592]{0:T(1024)(128)(4,1)} %bitcast.12), calls=%async_computation.3 | async-start | bytes 1048576
  31.8 70.2 %slice-start.1 = ((s8[4718592]{0:T(1024)(128)(4,1)}), s8[4194304]{0:T(1024)(128)(4,1)S(1)}, s32[]{:S(2)}) async-start(s8[4718592]{0:T(1024)(128)(4,1)} %bitcast.12), calls=%async_computation.4 | async-start | bytes 8388608

commit v5 on v4

--- a/solution.py
+++ b/solution.py
@@ -20,12 +20,14 @@
 
 
 def make_table(freq_count, sample_count):
-    freq_ids = lax.broadcasted_iota(jnp.int32, (freq_count, sample_count), 0)
-    sample_ids = lax.broadcasted_iota(jnp.int32, (freq_count, sample_count), 1)
-    phase_ids = freq_ids * sample_ids % sample_count
+    row_ids = lax.broadcasted_iota(jnp.int32, (2 * freq_count, sample_count), 0)
+    sample_ids = lax.broadcasted_iota(jnp.int32, (2 * freq_count, sample_count), 1)
+    phase_ids = row_ids // 2 * sample_ids % sample_count
     angles = phase_ids.astype(F32) * (2.0 * math.pi / sample_count)
     amplitude = 1.0 / math.sqrt(GATE)
-    return jnp.stack([jnp.cos(angles) * amplitude, -jnp.sin(angles) * amplitude]).astype(BF)
+    return jnp.where(
+        row_ids % 2 == 0, jnp.cos(angles) * amplitude, -jnp.sin(angles) * amplitude
+    ).astype(BF)
 
 
 def params(mib=56):
@@ -221,36 +223,25 @@
 
 
 def response_kernel(
-    place_ref, c_hbm, u_ref, u_hbm, band_ref, minus_hbm, plus_hbm, gram_ref,
-    c_ref, cb_ref, ub_ref, z_ref, acc, sems,
+    place_ref, c_ref, u_ref, u_hbm, band_ref, minus_hbm, plus_hbm, gram_ref, cb_ref, ub_ref, z_ref, sems
 ):
     all_cols = u_hbm.shape[1]
-    owners = c_hbm.shape[0]
+    owners = c_ref.shape[0]
     place = place_ref[0]
-    parts = ((0, owners // 2), (owners // 2, owners - owners // 2))
-
-    def arrivals(i, g):
-        first, count = parts[g]
-        pairs = [
-            (c_hbm.at[pl.ds(first, count), pl.ds(3 * i, 3)], c_ref.at[i, pl.ds(first, count)]),
+
+    def arrivals(i):
+        cols = [jnp.clip(place * 3 + i + n - 1, 0, all_cols - 1) for n in range(3)]
+        return [
+            pltpu.make_async_copy(
+                u_hbm.at[i, cols[n], :, pl.ds(HALF, HALF), :], ub_ref.at[i, n], sems.at[i, n]
+            )
+            for n in range(3)
         ]
-        if g == 1:
-            for n in range(3):
-                col = jnp.clip(place * 3 + i + n - 1, 0, all_cols - 1)
-                pairs.append((u_hbm.at[i, col, :, pl.ds(HALF, HALF), :], ub_ref.at[i, n]))
-            if i == 0:
-                below = jnp.maximum(place - 1, 0)
-                pairs.append((c_hbm.at[below, 9], cb_ref.at[i, 0]))
-            if i == 2:
-                above = jnp.minimum(place + 1, owners - 1)
-                pairs.append((c_hbm.at[above, 9], cb_ref.at[i, 2]))
-        at = [2 * g + k for k in range(len(pairs))]
-        return [pltpu.make_async_copy(s, d, sems.at[i, k]) for k, (s, d) in zip(at, pairs)]
 
     def sends(i):
         lanes = pl.ds(i * TILE, TILE)
         return [
-            pltpu.make_async_copy(z_ref.at[i, n], ref.at[0, :, :, lanes], sems.at[i, 8 + n])
+            pltpu.make_async_copy(z_ref.at[i, n], ref.at[0, :, :, lanes], sems.at[i, 3 + n])
             for n, ref in enumerate((minus_hbm, plus_hbm))
         ]
 
@@ -260,37 +251,22 @@
         left = left.reshape(depth, 512)
         return lax.dot_general(left, right, (((0,), (0,)), ((), ())), preferred_element_type=F32)
 
-    for g in range(2):
-        for copy in arrivals(0, g):
+    for i in range(3):
+        for copy in arrivals(i):
             copy.start()
+    below = c_ref[jnp.maximum(place - 1, 0), 9]
+    above = c_ref[jnp.minimum(place + 1, owners - 1), 9]
     for i in range(3):
         for n in range(3):
-            if (i, n) not in ((0, 0), (2, 2)):
-                cb_ref[i, n] = band_ref[i, n]
+            cb_ref[i, n] = band_ref[i, n]
         cb_ref[i, 3] = jnp.zeros((HALF, 512), BF)
         ub_ref[i, 3] = jnp.zeros((2, HALF, TILE), BF)
+    cb_ref[0, 0] = jnp.where(place > 0, below, jnp.zeros((), BF))
+    cb_ref[2, 2] = jnp.where(place < owners - 1, above, jnp.zeros((), BF))
     for i in range(3):
-        if i < 2:
-            for g in range(2):
-                for copy in arrivals(i + 1, g):
-                    copy.start()
-        for copy in arrivals(i, 0):
+        prod = product(c_ref[:, 3 * i : 3 * i + 3].reshape(3 * owners, HALF, 512), u_ref[i])
+        for copy in arrivals(i):
             copy.wait()
-        if i == 0:
-            mid = owners // 2
-            acc[...] = product(c_ref[0, :mid].reshape(3 * mid, HALF, 512), u_ref[0, : 3 * mid])
-        for copy in arrivals(i, 1):
-            copy.wait()
-        if i == 0:
-            cb_ref[0, 0] = jnp.where(place > 0, cb_ref[0, 0], jnp.zeros((), BF))
-        if i == 2:
-            cb_ref[2, 2] = jnp.where(place < owners - 1, cb_ref[2, 2], jnp.zeros((), BF))
-        first = owners // 2 if i == 0 else 0
-        prod = product(
-            c_ref[i, first:].reshape(3 * (owners - first), HALF, 512), u_ref[i, 3 * first :]
-        )
-        if i == 0:
-            prod += acc[...]
         prod += product(cb_ref[i], ub_ref[i])
         re = (prod[:256, :256] - prod[256:, 256:]).astype(BF)
         im = prod[256:, :256] + prod[:256, 256:]
@@ -323,15 +299,13 @@
     anywhere = pl.BlockSpec(memory_space=pl.ANY)
     return pl.pallas_call(
         response_kernel,
-        in_specs=[pl.BlockSpec(memory_space=pltpu.SMEM), anywhere, whole, anywhere, whole],
+        in_specs=[pl.BlockSpec(memory_space=pltpu.SMEM), whole, whole, anywhere, whole],
         out_specs=[anywhere, anywhere, whole],
         scratch_shapes=[
-            pltpu.VMEM((rows, all_cols // 3, 3, HALF, 512), BF),
             pltpu.VMEM((rows, 4, HALF, 512), BF),
             pltpu.VMEM((rows, 4, 2, HALF, TILE), BF),
             pltpu.VMEM((rows, 2, 2, 128, TILE), BF),
-            pltpu.VMEM((512, 512), F32),
-            pltpu.SemaphoreType.DMA((3, 10)),
+            pltpu.SemaphoreType.DMA((3, 5)),
         ],
         out_shape=[
             jax.ShapeDtypeStruct((1, 2, 128, rows * TILE), BF),
@@ -348,8 +322,7 @@
 def on_device(plus_time, minus_time, gate_starts, tile_ranks, u_factors, v_factors):
     u_factors, v_factors, ranks = u_factors[0], v_factors[0], tile_ranks[0].T
     place = lax.axis_index(TILES).astype(jnp.int32).reshape(1)
-    rows = make_table(8, 128).astype(F32).transpose(1, 0, 2)
-    local_spec = dft(plus_time, minus_time, gate_starts.T, rows.reshape(16, 128))
+    local_spec = dft(plus_time, minus_time, gate_starts.T, make_table(8, 128).astype(F32))
     spectra = lax.all_to_all(local_spec, FREQ, 0, 0, tiled=True)
     spectra, u_held = lax.optimization_barrier((spectra, held(u_factors)))
     coeffs, band = coefficients(spectra, v_factors, ranks, place)

time: 122 us -> 123 us (level)
  no operation moved by 1% of the time
where the time goes in v5:
time: 123 us; the launch traced here: 122 us
  blocking collectives  82 us (67%)
  Pallas kernels  22.8 us (19%)
  waiting for transfers between devices  8.63 us (7%)
  starting transfers between devices  4.41 us (4%)
  local copies, waits for them, and re-layouts  2.77 us (2%)
    all_to_all x1, blocking collectives, on_device(): arrived = lax.all_to_all(coeffs, TILES, 0, 0, tiled=True)  70.2 us
    all_to_all x1, blocking collectives, on_device(): sums = lax.all_to_all(gram, TILES, 0, 0, tiled=True).sum(axis=0)  11.8 us
    all_to_all x1, waiting for transfers between devices, on_device(): spectra = lax.all_to_all(local_spec, FREQ, 0, 0, tiled=True)  8.63 us
    pallas_call x1, Pallas kernels, respond(): pl.pallas_call(response_kernel, in_specs=[pl.BlockSpec(memory_space=pltpu...  7.54 us
    pallas_call x1, Pallas kernels, coefficients(): pl.pallas_call(coeff_kernel, in_specs=[scalars, scalars, whole, pl.BlockS...  7.46 us
    pallas_call x1, Pallas kernels, dft(): pl.pallas_call(dft_kernel, grid=(blocks,), in_specs=[pl.BlockSpec(memory_...  5.46 us
    all_to_all x1, starting transfers between devices, on_device(): spectra = lax.all_to_all(local_spec, FREQ, 0, 0, tiled=True)  4.41 us
  transfers between devices with their start and end apart: 1, of which 1 were waited for; matrix products, arithmetic and copies ran while one was open for 0% of the time, Pallas kernels for 2%

profile of v5, /device:TPU:0, one launch (start us, length us, event | category | flops | bytes accessed | tf_op | source)
XLA Modules:
  0.0 122.1 jit_solution(7318670093927929389)
XLA Ops:
  0.6 0.0 copy-start.1
  0.7 0.7 fusion.3.tab_ref
  1.4 5.5 %shard_map.93 = bf16[8,2,2,16,768]{4,3,2,1,0:T(8,128)(2,1)} custom-call(s32[3,16]{1,0:T(4,128)} %bitcast.15, f32[16,128]{1,0:T(8,128)} %fusion.3.tab_ref, bf16[16,128,768]{2,1,0:T(8,128)(2,1)} %plus_ref.1, bf16[16,128,768]{2,1,0:T(8,128)(2,1)} %minus_ref.1), custom_call_target="tpu_custom_call" | custom-call | flops 1610612736 | bytes 7340032 | tf_op jit(solution)/shard_map/pallas_call | solution.py:67
  6.9 4.4 %all-to-all-start = ((bf16[8,2,2,16,768]{4,3,2,1,0:T(8,128)(2,1)}), bf16[8,2,2,16,768]{4,3,2,1,0:T(8,128)(2,1)S(1)}, u32[]{:S(2)}, u32[]{:S(2)}) async-start(bf16[8,2,2,16,768]{4,3,2,1,0:T(8,128)(2,1)} %shard_map.93), calls=%async_computation | async-start | bytes 1572864 | tf_op jit(solution)/shard_map/all_to_all | solution.py:326
  11.3 0.0 copy-done.1
  11.3 2.3 %shard_map.94.u_ref = bf16[3,48,2,32,256]{4,3,2,1,0:T(8,128)(2,1)S(1)} custom-call(bf16[3,48,2,64,256]{4,3,2,1,0:T(8,128)(2,1)} %bitcast.12), custom_call_target="tpu_custom_call" | custom-call | bytes 5242880 | tf_op jit(solution)/shard_map/pallas_call | solution.py:93
  13.6 0.0 copy-start
  13.7 2.1 %copy-done = bf16[3,48,2,32,256]{4,3,2,1,0:T(8,128)(2,1)} copy-done((bf16[3,48,2,32,256]{4,3,2,1,0:T(8,128)(2,1)}, bf16[3,48,2,32,256]{4,3,2,1,0:T(8,128)(2,1)S(1)}, u32[]{:S(2)}) %copy-start) | copy-done | bytes 4718616
  15.8 8.6 %all-to-all-done.x_ref = bf16[8,2,2,16,768]{4,3,2,1,0:T(8,128)(2,1)S(1)} async-done(((bf16[8,2,2,16,768]{4,3,2,1,0:T(8,128)(2,1)}), bf16[8,2,2,16,768]{4,3,2,1,0:T(8,128)(2,1)S(1)}, u32[]{:S(2)}, u32[]{:S(2)}) %all-to-all-start) | async-done | bytes 786464 | tf_op jit(solution)/shard_map/all_to_all | solution.py:326
  24.4 0.0 slice-start
  24.4 7.5 %shard_map.95 = (bf16[16,10,32,512]{3,2,1,0:T(8,128)(2,1)}, bf16[3,3,32,512]{3,2,1,0:T(8,128)(2,1)S(1)}) custom-call(s32[1]{0:T(128)} %bitcast.place_ref, s32[3,48]{1,0:T(4,128)S(1)} %bitcast.11, bf16[8,2,2,16,768]{4,3,2,1,0:T(8,128)(2,1)S(1)} %all-to-all-done.x_ref, bf16[48,3,2,64,256]{4,3,2,1,0:T(8,128)(2,1)} %bitcast.14), custom_call_target="tpu_custom_call" | custom-call | flops 2415919104 | bytes 10485760 | tf_op jit(solution)/shard_map/pallas_call | solution.py:202
  31.9 0.0 slice-start.1
  31.9 70.2 %all_to_all.15.c_ref = bf16[16,10,32,512]{3,2,1,0:T(8,128)(2,1)S(1)} all-to-all(bf16[16,10,32,512]{3,2,1,0:T(8,128)(2,1)} %get-tuple-element.12), channel_id=1, replica_groups=mesh['fx'=4,'fc'=2,'ty'=4,'tz'=4] {'ty','tz'}, dimensions={0} | all-to-all | bytes 10485760 | tf_op jit(solution)/shard_map/all_to_all | solution.py:329
  102.1 0.0 slice-done
  102.1 0.0 slice-done.1
  102.1 7.5 %shard_map.96 = (bf16[1,2,128,768]{3,2,1,0:T(8,128)(2,1)}, bf16[1,2,128,768]{3,2,1,0:T(8,128)(2,1)}, f32[16,2,2,8,128]{4,3,2,1,0:T(8,128)S(1)}) custom-call(s32[1]{0:T(128)} %bitcast.place_ref, bf16[16,10,32,512]{3,2,1,0:T(8,128)(2,1)S(1)} %all_to_all.15.c_ref, bf16[3,48,2,32,256]{4,3,2,1,0:T(8,128)(2,1)S(1)} %bitcast.10, ...), custom_call_target="tpu_custom_call" | custom-call | flops 2415919104 | bytes 11534336 | tf_op jit(solution)/shard_map/pallas_call | solution.py:300
  109.7 11.8 %all_to_all.16 = f32[16,2,2,8,128]{4,3,2,1,0:T(8,128)S(1)} all-to-all(f32[16,2,2,8,128]{4,3,2,1,0:T(8,128)S(1)} %get-tuple-element.17), channel_id=1, replica_groups=mesh['fx'=4,'fc'=2,'ty'=4,'tz'=4] {'ty','tz'}, dimensions={0} | all-to-all | bytes 524288 | tf_op jit(solution)/shard_map/all_to_all | solution.py:331
  121.5 0.6 fusion.4
  (6 shorter events, 0.0 us)
Async XLA Ops:
  0.6 10.6 %copy-start.1 = (s32[1,48,3]{1,0,2:T(1,128)S(1)}, s32[1,48,3]{1,0,2:T(1,128)}, u32[]{:S(2)}) copy-start(s32[1,48,3]{1,0,2:T(1,128)} %param.9) | copy-start | bytes 1732
  6.9 17.6 %all-to-all-start = ((bf16[8,2,2,16,768]{4,3,2,1,0:T(8,128)(2,1)}), bf16[8,2,2,16,768]{4,3,2,1,0:T(8,128)(2,1)S(1)}, u32[]{:S(2)}, u32[]{:S(2)}) async-start(bf16[8,2,2,16,768]{4,3,2,1,0:T(8,128)(2,1)} %shard_map.93), calls=%async_computation | async-start | bytes 1572864 | tf_op jit(solution)/shard_map/all_to_all | solution.py:326
  13.6 2.2 %copy-start = (bf16[3,48,2,32,256]{4,3,2,1,0:T(8,128)(2,1)}, bf16[3,48,2,32,256]{4,3,2,1,0:T(8,128)(2,1)S(1)}, u32[]{:S(2)}) copy-start(bf16[3,48,2,32,256]{4,3,2,1,0:T(8,128)(2,1)S(1)} %shard_map.94.u_ref) | copy-start | bytes 14155780
  24.4 77.7 %slice-start = ((s8[4718592]{0:T(1024)(128)(4,1)}), s8[524288]{0:T(1024)(128)(4,1)S(1)}, s32[]{:S(2)}) async-start(s8[4718592]{0:T(1024)(128)(4,1)} %bitcast.9), calls=%async_computation.3 | async-start | bytes 1048576
  31.9 70.2 %slice-start.1 = ((s8[4718592]{0:T(1024)(128)(4,1)}), s8[4194304]{0:T(1024)(128)(4,1)S(1)}, s32[]{:S(2)}) async-start(s8[4718592]{0:T(1024)(128)(4,1)} %bitcast.9), calls=%async_computation.4 | async-start | bytes 8388608

commit v6 on v5

--- a/solution.py
+++ b/solution.py
@@ -263,10 +263,7 @@
         ub_ref[i, 3] = jnp.zeros((2, HALF, TILE), BF)
     cb_ref[0, 0] = jnp.where(place > 0, below, jnp.zeros((), BF))
     cb_ref[2, 2] = jnp.where(place < owners - 1, above, jnp.zeros((), BF))
-    for i in range(3):
-        prod = product(c_ref[:, 3 * i : 3 * i + 3].reshape(3 * owners, HALF, 512), u_ref[i])
-        for copy in arrivals(i):
-            copy.wait()
+    def settle(i, prod):
         prod += product(cb_ref[i], ub_ref[i])
         re = (prod[:256, :256] - prod[256:, 256:]).astype(BF)
         im = prod[256:, :256] + prod[:256, 256:]
@@ -275,8 +272,22 @@
         z_ref[i, 0, 1] = im[:128]
         z_ref[i, 1, 0] = re[128:]
         z_ref[i, 1, 1] = im[128:]
-        for copy in sends(i):
-            copy.start()
+
+    last = None
+    for i in range(3):
+        prod = product(c_ref[:, 3 * i : 3 * i + 3].reshape(3 * owners, HALF, 512), u_ref[i])
+        if i == 0:
+            for n in range(3):
+                for copy in arrivals(n):
+                    copy.wait()
+        else:
+            settle(i - 1, last)
+            for copy in sends(i - 1):
+                copy.start()
+        last = prod
+    settle(2, last)
+    for copy in sends(2):
+        copy.start()
     rows = [jnp.concatenate([z_ref[i, m, c] for i in range(3)], axis=1) for c in range(2) for m in range(2)]
     gram = lax.dot_general(
         jnp.concatenate(rows, axis=0),

time: 123 us -> 120 us (0.976)
  Pallas kernels: 22.8 us -> 20.3 us
    pallas_call x1, Pallas kernels: 7.54 us -> 5.05 us  [respond(): pl.pallas_call(response_kernel, in_specs=[pl.BlockSpec(memory_space=pltpu...]
where the time goes in v6:
time: 120 us
  blocking collectives  82 us (68%)
  Pallas kernels  20.3 us (17%)
  waiting for transfers between devices  8.63 us (7%)
  starting transfers between devices  4.41 us (4%)
  local copies, waits for them, and re-layouts  2.77 us (2%)
    all_to_all x1, blocking collectives, on_device(): arrived = lax.all_to_all(coeffs, TILES, 0, 0, tiled=True)  70.2 us
    all_to_all x1, blocking collectives, on_device(): sums = lax.all_to_all(gram, TILES, 0, 0, tiled=True).sum(axis=0)  11.8 us
    all_to_all x1, waiting for transfers between devices, on_device(): spectra = lax.all_to_all(local_spec, FREQ, 0, 0, tiled=True)  8.63 us
    pallas_call x1, Pallas kernels, coefficients(): pl.pallas_call(coeff_kernel, in_specs=[scalars, scalars, whole, pl.BlockS...  7.46 us
    pallas_call x1, Pallas kernels, dft(): pl.pallas_call(dft_kernel, grid=(blocks,), in_specs=[pl.BlockSpec(memory_...  5.46 us
    pallas_call x1, Pallas kernels, respond(): pl.pallas_call(response_kernel, in_specs=[pl.BlockSpec(memory_space=pltpu...  5.05 us
    all_to_all x1, starting transfers between devices, on_device(): spectra = lax.all_to_all(local_spec, FREQ, 0, 0, tiled=True)  4.41 us
  transfers between devices with their start and end apart: 1, of which 1 were waited for; matrix products, arithmetic and copies ran while one was open for 0% of the time, Pallas kernels for 2%

profile of v6, /device:TPU:0, one launch (start us, length us, event | category | flops | bytes accessed | tf_op | source)
XLA Modules:
  0.0 119.6 jit_solution(11864079978075688644)
XLA Ops:
  0.6 0.0 copy-start.1
  0.7 0.7 fusion.3.tab_ref
  1.4 5.5 %shard_map.93 = bf16[8,2,2,16,768]{4,3,2,1,0:T(8,128)(2,1)} custom-call(s32[3,16]{1,0:T(4,128)} %bitcast.15, f32[16,128]{1,0:T(8,128)} %fusion.3.tab_ref, bf16[16,128,768]{2,1,0:T(8,128)(2,1)} %plus_ref.1, bf16[16,128,768]{2,1,0:T(8,128)(2,1)} %minus_ref.1), custom_call_target="tpu_custom_call" | custom-call | flops 1610612736 | bytes 7340032 | tf_op jit(solution)/shard_map/pallas_call | solution.py:67
  6.9 4.4 %all-to-all-start = ((bf16[8,2,2,16,768]{4,3,2,1,0:T(8,128)(2,1)}), bf16[8,2,2,16,768]{4,3,2,1,0:T(8,128)(2,1)S(1)}, u32[]{:S(2)}, u32[]{:S(2)}) async-start(bf16[8,2,2,16,768]{4,3,2,1,0:T(8,128)(2,1)} %shard_map.93), calls=%async_computation | async-start | bytes 1572864 | tf_op jit(solution)/shard_map/all_to_all | solution.py:337
  11.3 0.0 copy-done.1
  11.3 2.3 %shard_map.94.u_ref = bf16[3,48,2,32,256]{4,3,2,1,0:T(8,128)(2,1)S(1)} custom-call(bf16[3,48,2,64,256]{4,3,2,1,0:T(8,128)(2,1)} %bitcast.12), custom_call_target="tpu_custom_call" | custom-call | bytes 5242880 | tf_op jit(solution)/shard_map/pallas_call | solution.py:93
  13.6 0.0 copy-start
  13.7 2.1 %copy-done = bf16[3,48,2,32,256]{4,3,2,1,0:T(8,128)(2,1)} copy-done((bf16[3,48,2,32,256]{4,3,2,1,0:T(8,128)(2,1)}, bf16[3,48,2,32,256]{4,3,2,1,0:T(8,128)(2,1)S(1)}, u32[]{:S(2)}) %copy-start) | copy-done | bytes 4718616
  15.8 8.6 %all-to-all-done.x_ref = bf16[8,2,2,16,768]{4,3,2,1,0:T(8,128)(2,1)S(1)} async-done(((bf16[8,2,2,16,768]{4,3,2,1,0:T(8,128)(2,1)}), bf16[8,2,2,16,768]{4,3,2,1,0:T(8,128)(2,1)S(1)}, u32[]{:S(2)}, u32[]{:S(2)}) %all-to-all-start) | async-done | bytes 786464 | tf_op jit(solution)/shard_map/all_to_all | solution.py:337
  24.4 0.0 slice-start
  24.4 7.5 %shard_map.95 = (bf16[16,10,32,512]{3,2,1,0:T(8,128)(2,1)}, bf16[3,3,32,512]{3,2,1,0:T(8,128)(2,1)S(1)}) custom-call(s32[1]{0:T(128)} %bitcast.place_ref, s32[3,48]{1,0:T(4,128)S(1)} %bitcast.11, bf16[8,2,2,16,768]{4,3,2,1,0:T(8,128)(2,1)S(1)} %all-to-all-done.x_ref, bf16[48,3,2,64,256]{4,3,2,1,0:T(8,128)(2,1)} %bitcast.14), custom_call_target="tpu_custom_call" | custom-call | flops 2415919104 | bytes 10485760 | tf_op jit(solution)/shard_map/pallas_call | solution.py:202
  31.9 0.0 slice-start.1
  31.9 70.2 %all_to_all.15.c_ref = bf16[16,10,32,512]{3,2,1,0:T(8,128)(2,1)S(1)} all-to-all(bf16[16,10,32,512]{3,2,1,0:T(8,128)(2,1)} %get-tuple-element.12), channel_id=1, replica_groups=mesh['fx'=4,'fc'=2,'ty'=4,'tz'=4] {'ty','tz'}, dimensions={0} | all-to-all | bytes 10485760 | tf_op jit(solution)/shard_map/all_to_all | solution.py:340
  102.1 0.0 slice-done
  102.1 0.0 slice-done.1
  102.1 5.0 %shard_map.96 = (bf16[1,2,128,768]{3,2,1,0:T(8,128)(2,1)}, bf16[1,2,128,768]{3,2,1,0:T(8,128)(2,1)}, f32[16,2,2,8,128]{4,3,2,1,0:T(8,128)S(1)}) custom-call(s32[1]{0:T(128)} %bitcast.place_ref, bf16[16,10,32,512]{3,2,1,0:T(8,128)(2,1)S(1)} %all_to_all.15.c_ref, bf16[3,48,2,32,256]{4,3,2,1,0:T(8,128)(2,1)S(1)} %bitcast.10, ...), custom_call_target="tpu_custom_call" | custom-call | flops 2415919104 | bytes 11534336 | tf_op jit(solution)/shard_map/pallas_call | solution.py:311
  107.2 11.8 %all_to_all.16 = f32[16,2,2,8,128]{4,3,2,1,0:T(8,128)S(1)} all-to-all(f32[16,2,2,8,128]{4,3,2,1,0:T(8,128)S(1)} %get-tuple-element.17), channel_id=1, replica_groups=mesh['fx'=4,'fc'=2,'ty'=4,'tz'=4] {'ty','tz'}, dimensions={0} | all-to-all | bytes 524288 | tf_op jit(solution)/shard_map/all_to_all | solution.py:342
  119.0 0.6 fusion.4
  (6 shorter events, 0.0 us)
Async XLA Ops:
  0.6 10.6 %copy-start.1 = (s32[1,48,3]{1,0,2:T(1,128)S(1)}, s32[1,48,3]{1,0,2:T(1,128)}, u32[]{:S(2)}) copy-start(s32[1,48,3]{1,0,2:T(1,128)} %param.9) | copy-start | bytes 1732
  6.9 17.6 %all-to-all-start = ((bf16[8,2,2,16,768]{4,3,2,1,0:T(8,128)(2,1)}), bf16[8,2,2,16,768]{4,3,2,1,0:T(8,128)(2,1)S(1)}, u32[]{:S(2)}, u32[]{:S(2)}) async-start(bf16[8,2,2,16,768]{4,3,2,1,0:T(8,128)(2,1)} %shard_map.93), calls=%async_computation | async-start | bytes 1572864 | tf_op jit(solution)/shard_map/all_to_all | solution.py:337
  13.6 2.2 %copy-start = (bf16[3,48,2,32,256]{4,3,2,1,0:T(8,128)(2,1)}, bf16[3,48,2,32,256]{4,3,2,1,0:T(8,128)(2,1)S(1)}, u32[]{:S(2)}) copy-start(bf16[3,48,2,32,256]{4,3,2,1,0:T(8,128)(2,1)S(1)} %shard_map.94.u_ref) | copy-start | bytes 14155780
  24.4 77.7 %slice-start = ((s8[4718592]{0:T(1024)(128)(4,1)}), s8[524288]{0:T(1024)(128)(4,1)S(1)}, s32[]{:S(2)}) async-start(s8[4718592]{0:T(1024)(128)(4,1)} %bitcast.9), calls=%async_computation.3 | async-start | bytes 1048576
  31.9 70.2 %slice-start.1 = ((s8[4718592]{0:T(1024)(128)(4,1)}), s8[4194304]{0:T(1024)(128)(4,1)S(1)}, s32[]{:S(2)}) async-start(s8[4718592]{0:T(1024)(128)(4,1)} %bitcast.9), calls=%async_computation.4 | async-start | bytes 8388608

commit v7 on v6

--- a/solution.py
+++ b/solution.py
@@ -83,22 +83,31 @@
     )(gate_starts, table, plus_time, minus_time)
 
 
-def hold_kernel(u_hbm, u_ref, sem):
-    copy = pltpu.make_async_copy(u_hbm.at[:, :, :, pl.ds(0, HALF), :], u_ref, sem)
-    copy.start()
-    copy.wait()
-
-
-def held(u_factors):
+def hold_kernel(u_hbm, v_hbm, u_ref, v_ref, sems):
+    low = pl.ds(0, HALF)
+    copies = [
+        pltpu.make_async_copy(v_hbm.at[:, :, :, low, :], v_ref, sems.at[0]),
+        pltpu.make_async_copy(u_hbm.at[:, :, :, low, :], u_ref, sems.at[1]),
+    ]
+    for copy in copies:
+        copy.start()
+    for copy in copies:
+        copy.wait()
+
+
+def held(u_factors, v_factors):
+    anywhere = pl.BlockSpec(memory_space=pl.ANY)
+    whole = pl.BlockSpec(memory_space=pltpu.VMEM)
+    shapes = [(*f.shape[:3], HALF, TILE) for f in (u_factors, v_factors)]
     return pl.pallas_call(
         hold_kernel,
-        in_specs=[pl.BlockSpec(memory_space=pl.ANY)],
-        out_specs=pl.BlockSpec(memory_space=pltpu.VMEM),
-        out_shape=pltpu.VMEM((*u_factors.shape[:3], HALF, TILE), BF),
-        scratch_shapes=[pltpu.SemaphoreType.DMA],
-        compiler_params=params(52),
-        cost_estimate=pl.CostEstimate(flops=0, bytes_accessed=5 * 2**20, transcendentals=0),
-    )(u_factors)
+        in_specs=[anywhere, anywhere],
+        out_specs=[whole, whole],
+        out_shape=[jax.ShapeDtypeStruct(shape, BF) for shape in shapes],
+        scratch_shapes=[pltpu.SemaphoreType.DMA((2,))],
+        compiler_params=params(44),
+        cost_estimate=pl.CostEstimate(flops=0, bytes_accessed=10 * 2**20, transcendentals=0),
+    )(u_factors, v_factors)
 
 
 def fill_weights(w_ref, x_ref):
@@ -113,15 +122,14 @@
 
 
 def coeff_kernel(
-    place_ref, ranks_ref, x_ref, v_hbm, out_hbm, band_ref, v_ref, b_ref, o_ref, e_ref, w_ref, sems
+    place_ref, ranks_ref, x_ref, v_ref, v_hbm, out_hbm, band_ref, b_ref, o_ref, e_ref, w_ref, sems
 ):
     last_row = v_hbm.shape[0] - 1
     owners = out_hbm.shape[0]
     place = place_ref[0]
 
     def arrivals(j):
-        low = v_hbm.at[:, j, :, pl.ds(0, HALF), :]
-        copies = [pltpu.make_async_copy(low, v_ref.at[j], sems.at[j, 0])]
+        copies = []
         for n in range(3):
             i = jnp.clip(place * 3 + j + n - 1, 0, last_row)
             src = v_hbm.at[i, j, :, pl.ds(HALF, HALF), :]
@@ -165,7 +173,7 @@
                 band_ref[il, 2 - n] = kept
         for h in range(4):
             rows = slice(h * 12, (h + 1) * 12)
-            v = jnp.concatenate([v_ref[j, rows, c].reshape(12 * HALF, TILE) for c in range(2)], axis=1)
+            v = jnp.concatenate([v_ref[rows, j, c].reshape(12 * HALF, TILE) for c in range(2)], axis=1)
             prod = jnp.dot(v, w_ref[...], preferred_element_type=F32)
             for n in range(12):
                 i = h * 12 + n
@@ -195,31 +203,30 @@
         edge(1).wait()
 
 
-def coefficients(spectra, v_factors, ranks, place):
+def coefficients(spectra, v_held, v_factors, ranks, place):
     rows, cols = v_factors.shape[:2]
     whole = pl.BlockSpec(memory_space=pltpu.VMEM)
     scalars = pl.BlockSpec(memory_space=pltpu.SMEM)
     return pl.pallas_call(
         coeff_kernel,
-        in_specs=[scalars, scalars, whole, pl.BlockSpec(memory_space=pl.ANY)],
+        in_specs=[scalars, scalars, whole, whole, pl.BlockSpec(memory_space=pl.ANY)],
         out_specs=[pl.BlockSpec(memory_space=pl.ANY), whole],
         out_shape=[
             jax.ShapeDtypeStruct((rows // 3, 10, HALF, 512), BF),
             jax.ShapeDtypeStruct((3, 3, HALF, 512), BF),
         ],
         scratch_shapes=[
-            pltpu.VMEM((cols, rows, 2, HALF, TILE), BF),
             pltpu.VMEM((cols, 3, 2, HALF, TILE), BF),
             pltpu.VMEM((cols, 3, rows // 3, HALF, 512), BF),
             pltpu.VMEM((2, HALF, 512), BF),
             pltpu.VMEM((512, 512), BF),
             pltpu.SemaphoreType.DMA((3, 8)),
         ],
-        compiler_params=params(52),
+        compiler_params=params(40),
         cost_estimate=pl.CostEstimate(
             flops=2 * rows * cols * HALF * 512 * 512, bytes_accessed=10 * 2**20, transcendentals=0
         ),
-    )(place, ranks, spectra, v_factors)
+    )(place, ranks, spectra, v_held, v_factors)
 
 
 def response_kernel(
@@ -335,8 +342,9 @@
     place = lax.axis_index(TILES).astype(jnp.int32).reshape(1)
     local_spec = dft(plus_time, minus_time, gate_starts.T, make_table(8, 128).astype(F32))
     spectra = lax.all_to_all(local_spec, FREQ, 0, 0, tiled=True)
-    spectra, u_held = lax.optimization_barrier((spectra, held(u_factors)))
-    coeffs, band = coefficients(spectra, v_factors, ranks, place)
+    u_held, v_held = held(u_factors, v_factors)
+    spectra, u_held = lax.optimization_barrier((spectra, u_held))
+    coeffs, band = coefficients(spectra, v_held, v_factors, ranks, place)
     arrived = lax.all_to_all(coeffs, TILES, 0, 0, tiled=True)
     minus_new, plus_new, gram = respond(arrived, u_held, u_factors, band, place)
     sums = lax.all_to_all(gram, TILES, 0, 0, tiled=True).sum(axis=0)

time: 120 us -> 120 us (level)
  local copies, waits for them, and re-layouts: 2.77 us -> 7.27 us
  waiting for transfers between devices: 8.63 us -> 5.01 us
    unnamed x9 -> x11, local copies, waits for them, and re-layouts: 2.16 us -> 6.66 us
    all_to_all x1, waiting for transfers between devices: 8.63 us -> 5.01 us  [on_device(): spectra = lax.all_to_all(local_spec, FREQ, 0, 0, tiled=True)]
  transfers between devices with their start and end apart: 1 -> 1, of which waited for: 1 -> 1; matrix products, arithmetic and copies ran while one was open for 0% -> 0% of each run, Pallas kernels for 2% -> 3%
where the time goes in v7:
time: 120 us
  blocking collectives  81.7 us (68%)
  Pallas kernels  19.8 us (16%)
  local copies, waits for them, and re-layouts  7.27 us (6%)
  waiting for transfers between devices  5.01 us (4%)
  starting transfers between devices  4.41 us (4%)
    all_to_all x1, blocking collectives, on_device(): arrived = lax.all_to_all(coeffs, TILES, 0, 0, tiled=True)  70 us
    all_to_all x1, blocking collectives, on_device(): sums = lax.all_to_all(gram, TILES, 0, 0, tiled=True).sum(axis=0)  11.8 us
    unnamed x11, local copies, waits for them, and re-layouts  6.66 us
    pallas_call x1, Pallas kernels, coefficients(): pl.pallas_call(coeff_kernel, in_specs=[scalars, scalars, whole, whole, pl...  5.47 us
    pallas_call x1, Pallas kernels, dft(): pl.pallas_call(dft_kernel, grid=(blocks,), in_specs=[pl.BlockSpec(memory_...  5.45 us
    pallas_call x1, Pallas kernels, respond(): pl.pallas_call(response_kernel, in_specs=[pl.BlockSpec(memory_space=pltpu...  5.05 us
    all_to_all x1, waiting for transfers between devices, on_device(): spectra = lax.all_to_all(local_spec, FREQ, 0, 0, tiled=True)  5.01 us
    all_to_all x1, starting transfers between devices, on_device(): spectra = lax.all_to_all(local_spec, FREQ, 0, 0, tiled=True)  4.41 us
  transfers between devices with their start and end apart: 1, of which 1 were waited for; matrix products, arithmetic and copies ran while one was open for 0% of the time, Pallas kernels for 3%

profile of v7, /device:TPU:0, one launch (start us, length us, event | category | flops | bytes accessed | tf_op | source)
XLA Modules:
  0.0 119.7 jit_solution(6245128841695107978)
XLA Ops:
  0.6 0.0 copy-start.4
  0.7 0.7 fusion.3.tab_ref
  1.4 5.5 %shard_map.93 = bf16[8,2,2,16,768]{4,3,2,1,0:T(8,128)(2,1)} custom-call(s32[3,16]{1,0:T(4,128)} %bitcast.14, f32[16,128]{1,0:T(8,128)} %fusion.3.tab_ref, bf16[16,128,768]{2,1,0:T(8,128)(2,1)} %plus_ref.1, bf16[16,128,768]{2,1,0:T(8,128)(2,1)} %minus_ref.1), custom_call_target="tpu_custom_call" | custom-call | flops 1610612736 | bytes 7340032 | tf_op jit(solution)/shard_map/pallas_call | solution.py:67
  6.9 4.4 %all-to-all-start = ((bf16[8,2,2,16,768]{4,3,2,1,0:T(8,128)(2,1)}), bf16[8,2,2,16,768]{4,3,2,1,0:T(8,128)(2,1)S(1)}, u32[]{:S(2)}, u32[]{:S(2)}) async-start(bf16[8,2,2,16,768]{4,3,2,1,0:T(8,128)(2,1)} %shard_map.93), calls=%async_computation | async-start | bytes 1572864 | tf_op jit(solution)/shard_map/all_to_all | solution.py:344
  11.3 0.0 copy-done.4
  11.3 3.8 %shard_map.94 = (bf16[3,48,2,32,256]{4,3,2,1,0:T(8,128)(2,1)S(1)}, bf16[48,3,2,32,256]{4,3,2,1,0:T(8,128)(2,1)S(1)}) custom-call(bf16[3,48,2,64,256]{4,3,2,1,0:T(8,128)(2,1)} %bitcast.12, bf16[48,3,2,64,256]{4,3,2,1,0:T(8,128)(2,1)} %bitcast.10), custom_call_target="tpu_custom_call" | custom-call | bytes 10485760 | tf_op jit(solution)/shard_map/pallas_call | solution.py:102
  15.1 0.0 copy-start
  15.1 2.1 %copy-done = bf16[48,3,2,32,256]{4,3,2,1,0:T(8,128)(2,1)} copy-done((bf16[48,3,2,32,256]{4,3,2,1,0:T(8,128)(2,1)}, bf16[48,3,2,32,256]{4,3,2,1,0:T(8,128)(2,1)S(1)}, u32[]{:S(2)}) %copy-start) | copy-done | bytes 4718616
  17.2 0.0 copy-start.2
  17.2 2.2 %copy-done.2 = bf16[3,48,2,32,256]{4,3,2,1,0:T(8,128)(2,1)} copy-done((bf16[3,48,2,32,256]{4,3,2,1,0:T(8,128)(2,1)}, bf16[3,48,2,32,256]{4,3,2,1,0:T(8,128)(2,1)S(1)}, u32[]{:S(2)}) %copy-start.2) | copy-done | bytes 4718616
  19.4 5.0 %all-to-all-done.x_ref = bf16[8,2,2,16,768]{4,3,2,1,0:T(8,128)(2,1)S(1)} async-done(((bf16[8,2,2,16,768]{4,3,2,1,0:T(8,128)(2,1)}), bf16[8,2,2,16,768]{4,3,2,1,0:T(8,128)(2,1)S(1)}, u32[]{:S(2)}, u32[]{:S(2)}) %all-to-all-start) | async-done | bytes 786464 | tf_op jit(solution)/shard_map/all_to_all | solution.py:344
  24.4 0.0 copy-start.1
  24.4 2.3 %copy-done.1 = bf16[48,3,2,32,256]{4,3,2,1,0:T(8,128)(2,1)S(1)} copy-done((bf16[48,3,2,32,256]{4,3,2,1,0:T(8,128)(2,1)S(1)}, bf16[48,3,2,32,256]{4,3,2,1,0:T(8,128)(2,1)}, u32[]{:S(2)}) %copy-start.1) | copy-done | bytes 4718616
  26.8 5.5 %shard_map.95 = (bf16[16,10,32,512]{3,2,1,0:T(8,128)(2,1)S(1)}, bf16[3,3,32,512]{3,2,1,0:T(8,128)(2,1)S(1)}) custom-call(s32[1]{0:T(128)} %bitcast.place_ref, s32[3,48]{1,0:T(4,128)S(1)} %bitcast.9, bf16[8,2,2,16,768]{4,3,2,1,0:T(8,128)(2,1)S(1)} %all-to-all-done.x_ref, bf16[48,3,2,32,256]{4,3,2,1,0:T(8,128)(2,1)S(1)} %copy-done.1, ...), custom_call_target="tpu_custom_call" | custom-call | flops 2415919104 | bytes 10485760 | tf_op jit(solution)/shard_map/pallas_call | solution.py:210
  32.2 0.0 copy-start.3
  32.2 70.0 %all_to_all.15.c_ref = bf16[16,10,32,512]{3,2,1,0:T(8,128)(2,1)S(1)} all-to-all(bf16[16,10,32,512]{3,2,1,0:T(8,128)(2,1)S(1)} %get-tuple-element.16), channel_id=1, replica_groups=mesh['fx'=4,'fc'=2,'ty'=4,'tz'=4] {'ty','tz'}, dimensions={0} | all-to-all | bytes 10485760 | tf_op jit(solution)/shard_map/all_to_all | solution.py:348
  102.2 0.0 copy-done.3
  102.2 5.0 %shard_map.96 = (bf16[1,2,128,768]{3,2,1,0:T(8,128)(2,1)}, bf16[1,2,128,768]{3,2,1,0:T(8,128)(2,1)}, f32[16,2,2,8,128]{4,3,2,1,0:T(8,128)S(1)}) custom-call(s32[1]{0:T(128)} %bitcast.place_ref, bf16[16,10,32,512]{3,2,1,0:T(8,128)(2,1)S(1)} %all_to_all.15.c_ref, bf16[3,48,2,32,256]{4,3,2,1,0:T(8,128)(2,1)S(1)} %copy-done.3, ...), custom_call_target="tpu_custom_call" | custom-call | flops 2415919104 | bytes 11534336 | tf_op jit(solution)/shard_map/pallas_call | solution.py:318
  107.3 11.8 %all_to_all.16 = f32[16,2,2,8,128]{4,3,2,1,0:T(8,128)S(1)} all-to-all(f32[16,2,2,8,128]{4,3,2,1,0:T(8,128)S(1)} %get-tuple-element.21), channel_id=1, replica_groups=mesh['fx'=4,'fc'=2,'ty'=4,'tz'=4] {'ty','tz'}, dimensions={0} | all-to-all | bytes 524288 | tf_op jit(solution)/shard_map/all_to_all | solution.py:350
  119.1 0.6 fusion.4
  (5 shorter events, 0.0 us)
Async XLA Ops:
  0.6 10.6 %copy-start.4 = (s32[1,48,3]{1,0,2:T(1,128)S(1)}, s32[1,48,3]{1,0,2:T(1,128)}, u32[]{:S(2)}) copy-start(s32[1,48,3]{1,0,2:T(1,128)} %param.9) | copy-start | bytes 1732
  6.9 17.6 %all-to-all-start = ((bf16[8,2,2,16,768]{4,3,2,1,0:T(8,128)(2,1)}), bf16[8,2,2,16,768]{4,3,2,1,0:T(8,128)(2,1)S(1)}, u32[]{:S(2)}, u32[]{:S(2)}) async-start(bf16[8,2,2,16,768]{4,3,2,1,0:T(8,128)(2,1)} %shard_map.93), calls=%async_computation | async-start | bytes 1572864 | tf_op jit(solution)/shard_map/all_to_all | solution.py:344
  15.1 2.1 %copy-start = (bf16[48,3,2,32,256]{4,3,2,1,0:T(8,128)(2,1)}, bf16[48,3,2,32,256]{4,3,2,1,0:T(8,128)(2,1)S(1)}, u32[]{:S(2)}) copy-start(bf16[48,3,2,32,256]{4,3,2,1,0:T(8,128)(2,1)S(1)} %get-tuple-element.15.v_ref) | copy-start | bytes 14155780
  17.2 2.2 %copy-start.2 = (bf16[3,48,2,32,256]{4,3,2,1,0:T(8,128)(2,1)}, bf16[3,48,2,32,256]{4,3,2,1,0:T(8,128)(2,1)S(1)}, u32[]{:S(2)}) copy-start(bf16[3,48,2,32,256]{4,3,2,1,0:T(8,128)(2,1)S(1)} %get-tuple-element.17.u_ref) | copy-start | bytes 14155780
  24.4 2.3 %copy-start.1 = (bf16[48,3,2,32,256]{4,3,2,1,0:T(8,128)(2,1)S(1)}, bf16[48,3,2,32,256]{4,3,2,1,0:T(8,128)(2,1)}, u32[]{:S(2)}) copy-start(bf16[48,3,2,32,256]{4,3,2,1,0:T(8,128)(2,1)} %copy-done) | copy-start | bytes 14155780
  32.2 70.0 %copy-start.3 = (bf16[3,48,2,32,256]{4,3,2,1,0:T(8,128)(2,1)S(1)}, bf16[3,48,2,32,256]{4,3,2,1,0:T(8,128)(2,1)}, u32[]{:S(2)}) copy-start(bf16[3,48,2,32,256]{4,3,2,1,0:T(8,128)(2,1)} %copy-done.2) | copy-start | bytes 14155780
